TPU v7x, 256 devices: a whole 4x4x8 slice. The times are simulated.
256 devices in a mesh: row: 16 (over x, z_lo, core), col: 4 (over y), rep: 4 (over z_hi).
Axes of the slice: x: 4, y: 4, z: 8 (z_hi: 4, z_lo: 2; z = z_hi * 2 + z_lo), core: 2. Of those that a mesh axis runs over, the one named last changes fastest.
Arguments:
- a_values: float32 [16, 4, 4, 192, 128, 128], P('row', 'col', 'rep'), may hold values from -6 to 6
- b_values: float32 [16, 4, 4, 16, 128, 128], P('row', 'col', 'rep'), may hold values from -0.125 to 0.125
- a_live: int32 [16, 4, 4, 192], P('row', 'col', 'rep'), may hold values from 0 to 1, as said below
- b_live: int32 [16, 4, 4, 16], P('row', 'col', 'rep'), may hold values from 0 to 1, as said below
- triples: int32 [16, 4, 4, 2, 3, 256], P('row', 'col', 'rep'), may hold values from 0 to 191, as said below
Outputs:
- product_blocks: float32 [16, 4, 48, 128, 128], P('row', 'col', 'rep')
Inputs may be any that keep to these rules, and one draw needn't show every extreme that they name: `a_live`: each tile has at most 96 occupied slots and at least half as many; some tile has exactly 96. `b_live`: each tile has at most 8 occupied slots and at least half as many; some tile has exactly 8. `triples`: in each table the live entries come first, at least 64 of them; some table is full; left slots are below 192, right slots below 16, product slots at most 48; padding entries have product slot 48 and left and right slots 0.
All inputs are finite; a program needn't handle non-finite values.
Results may differ from a plain program's by a relative error of at most 0.0003.
Values sent between devices are 32-bit elements; how exact they have to be, the bound alone decides.
No kernel may reach another device: no remote copies, remote signals or barrier semaphores. Data moves between devices by JAX's collectives and lax.ppermute only.
A program may use at most 128 MiB of HBM per device.

v0:
```python
import math

import jax
import jax.numpy as jnp
from jax import lax
from jax.sharding import PartitionSpec as P

BS = 128
C_SLOTS = 48


def passed_along(x, axis, by):
    devices = lax.axis_size(axis)
    return lax.ppermute(x, axis, [(i, (i + by) % devices) for i in range(devices)])


def select_blocks(tile, indices):
    slots = tile.shape[0]
    block_order = tile.shape[1]
    chooser = (indices[:, None] == jnp.arange(slots, dtype=jnp.int32)[None, :]).astype(jnp.float32)
    flat = tile.reshape(slots, block_order * block_order)
    picked = jnp.dot(
        chooser, flat, precision=lax.Precision.HIGHEST, preferred_element_type=jnp.float32
    )
    return picked.reshape(indices.shape[0], block_order, block_order)


def group_products(left_tile, right_tile, triple_group, targets):
    left_blocks = select_blocks(left_tile, triple_group[0])
    right_blocks = select_blocks(right_tile, triple_group[1])
    block_products = jnp.einsum(
        "tik,tkj->tij",
        left_blocks,
        right_blocks,
        precision=lax.Precision.HIGHEST,
        preferred_element_type=jnp.float32,
    )
    placing = (triple_group[2][:, None] == targets).astype(jnp.float32)
    return jnp.einsum(
        "tc,tij->cij",
        placing,
        block_products,
        precision=lax.Precision.HIGHEST,
        preferred_element_type=jnp.float32,
    )


def batch_products(left_tile, right_tile, table, row_count):
    entries = table.shape[1]
    batch_width = math.gcd(entries, 128)
    groups = jnp.transpose(table.reshape(3, entries // batch_width, batch_width), (1, 0, 2))
    block_order = left_tile.shape[1]
    targets = jnp.arange(row_count, dtype=jnp.int32)[None, :]

    def advance(totals, triple_group):
        return (totals + group_products(left_tile, right_tile, triple_group, targets), None)

    initial = jnp.zeros((row_count, block_order, block_order), jnp.float32)
    totals, _ = lax.scan(advance, initial, groups)
    return totals


def shards(a_values, b_values, a_live, b_live, triples):
    left_here = a_values[0, 0, 0] * a_live[0, 0, 0][:, None, None].astype(jnp.float32)
    right_here = b_values[0, 0, 0] * b_live[0, 0, 0][:, None, None].astype(jnp.float32)
    tables_here = triples[0, 0, 0]
    left_next = passed_along(left_here, "row", -1)
    right_next = passed_along(right_here, "col", -1)
    share_rows = C_SLOTS // lax.axis_size("rep")
    first = batch_products(left_here, right_here, tables_here[0], C_SLOTS)
    second = batch_products(left_next, right_next, tables_here[1], C_SLOTS)
    shares = lax.psum_scatter(first + second, "rep", scatter_dimension=0, tiled=True)
    return shares.reshape(1, 1, share_rows, BS, BS)


def solution(mesh):
    placed = (
        P("row", "col", "rep", None, None, None),
        P("row", "col", "rep", None, None, None),
        P("row", "col", "rep", None),
        P("row", "col", "rep", None),
        P("row", "col", "rep", None, None, None),
    )
    return jax.shard_map(
        shards,
        mesh=mesh,
        in_specs=placed,
        out_specs=P("row", "col", "rep", None, None),
        check_vma=False,
    )
```

profile of v0, /device:TPU:8, one launch (start us, length us, event | category | flops | bytes accessed | tf_op | source)
XLA Modules:
  0.0 348.2 jit_solution(16974054357207610281)
XLA Ops:
  6.5 0.0 reduce-scatter.2.cloned.1.call-start
  6.5 0.7 convert_element_type.28
  7.2 0.0 copy-start.5
  7.2 0.0 copy-start.3
  7.2 0.0 copy-start.4
  7.2 10.0 %bitcast_multiply_fusion = f32[192,128,128]{2,1,0:T(8,128)} fusion(f32[1,1,1,192,128,128]{5,4,3,2,1,0:T(8,128)} %param.9, f32[192]{0:T(256)S(1)} %bitcast.159), kind=kLoop, calls=%fused_computation.60 | loop fusion | flops 3145728 | bytes 25166592 | tf_op jit(solution)/shard_map/mul | solution.py:64
  17.2 3.6 %collective-permute-start = (f32[192,128,128]{2,1,0:T(8,128)}, f32[192,128,128]{2,1,0:T(8,128)}, u32[]{:S(2)}, u32[]{:S(2)}) collective-permute-start(f32[192,128,128]{2,1,0:T(8,128)} %bitcast_multiply_fusion), channel_id=1, source_target_pairs={{0,240},{16,0},{32,16},{48,32},{64,48},{80,64},{96,80},{112,96},{1... | collective-permute-start | bytes 37748744 | tf_op jit(solution)/shard_map/ppermute | solution.py:14
  20.8 0.0 copy-done.5
  20.8 0.0 copy-done.3
  20.8 1.1 bitcast_multiply_fusion.1
  21.9 0.4 collective-permute-start.1
  22.4 0.0 copy-done.4
  22.4 133.1 %while.22 = (s32[]{:T(128)}, f32[48,128,128]{2,0,1:T(8,128)}, s32[2,3,128]{2,0,1:T(2,128)S(1)}, f32[192,128,128]{2,1,0:T(8,128)}, f32[16,128,128]{2,1,0:T(8,128)}, /*index=5*/s32[]{:T(128)}, s32[]{:T(128)}, s32[]{}, s32[]{}) while((s32[]{:T(128)}, f32[48,128,128]{2,0,1:T(8,128)}, s32[2,3,128]{2,0,1:T(2,128)S(1)}, ...), condition=%wide.region_1.2_spmd.clone, body=%wide.region_0.1_spmd.clone.sunk | while | flops 9665282048 | bytes 145756912 | solution.py:59
  22.6 0.0 copy-start
  22.6 4.9 %fusion.88 = f32[128,128,128]{2,0,1:T(8,128)S(1)} fusion(s32[128]{0:T(128)S(1)} %get-tuple-element.212, f32[2,8,128,128]{3,2,1,0:T(8,128)} %bitcast.142), kind=kOutput, calls=%fused_computation.13.clone.1 | convolution fusion | flops 402655232 | bytes 9437696 | tf_op jit(solution)/shard_map/while/body/eval_jaxpr/dot_general | solution.py:22
  27.5 0.0 copy-done
  27.5 18.1 %fusion.89 = f32[128,128,128]{2,0,1:T(8,128)} fusion(s32[128]{0:T(128)S(1)} %get-tuple-element.213, f32[24,8,128,128]{3,2,1,0:T(8,128)S(1)} %bitcast.156), kind=kOutput, calls=%fused_computation.3.clone.1 | convolution fusion | flops 4831862784 | bytes 20972032 | tf_op jit(solution)/shard_map/while/body/eval_jaxpr/dot_general | solution.py:22
  45.6 0.0 copy-start.1
  45.6 22.0 %fusion.90 = f32[128,128,128]{2,1,0:T(8,128)S(1)} fusion(f32[128,128,128]{2,0,1:T(8,128)S(1)} %fusion.88, f32[128,128,128]{2,0,1:T(8,128)} %fusion.89), kind=kOutput, calls=%fused_computation.8.clone.1 | convolution fusion | flops 3221225472 | bytes 25165824 | tf_op jit(solution)/shard_map/while/body/eval_jaxpr/tik,tkj->tij/dot_general | solution.py:31
  67.6 0.0 copy-done.1
  67.6 9.4 %select_add_fusion.4 = f32[48,128,128]{2,0,1:T(8,128)S(1)} fusion(f32[48,128,128]{2,0,1:T(8,128)S(1)} %copy-done.1, f32[128,128,128]{2,1,0:T(8,128)S(1)} %fusion.90, pred[]{:T(512)S(6)} %compare.6, s32[128]{0:T(128)S(1)} %get-tuple-element.214), kind=kOutput, calls=%fused_computation.11.clone.1 | convolution fusion | flops 1209538560 | bytes 14680577 | tf_op jit(solution)/shard_map/while/body/eval_jaxpr/tc,tij->cij/dot_general | solution.py:39
  77.0 0.0 copy-start.2
  77.0 1.6 copy-done.2
  78.6 0.0 copy-start
  78.6 4.9 %fusion.88 = f32[128,128,128]{2,0,1:T(8,128)S(1)} fusion(s32[128]{0:T(128)S(1)} %get-tuple-element.212, f32[2,8,128,128]{3,2,1,0:T(8,128)} %bitcast.142), kind=kOutput, calls=%fused_computation.13.clone.1 | convolution fusion | flops 402655232 | bytes 9437696 | tf_op jit(solution)/shard_map/while/body/eval_jaxpr/dot_general | solution.py:22
  83.5 0.0 copy-done
  83.5 18.1 %fusion.89 = f32[128,128,128]{2,0,1:T(8,128)} fusion(s32[128]{0:T(128)S(1)} %get-tuple-element.213, f32[24,8,128,128]{3,2,1,0:T(8,128)S(1)} %bitcast.156), kind=kOutput, calls=%fused_computation.3.clone.1 | convolution fusion | flops 4831862784 | bytes 20972032 | tf_op jit(solution)/shard_map/while/body/eval_jaxpr/dot_general | solution.py:22
  101.6 0.0 copy-start.1
  101.6 22.0 %fusion.90 = f32[128,128,128]{2,1,0:T(8,128)S(1)} fusion(f32[128,128,128]{2,0,1:T(8,128)S(1)} %fusion.88, f32[128,128,128]{2,0,1:T(8,128)} %fusion.89), kind=kOutput, calls=%fused_computation.8.clone.1 | convolution fusion | flops 3221225472 | bytes 25165824 | tf_op jit(solution)/shard_map/while/body/eval_jaxpr/tik,tkj->tij/dot_general | solution.py:31
  123.6 0.0 copy-done.1
  123.6 9.4 %select_add_fusion.4 = f32[48,128,128]{2,0,1:T(8,128)S(1)} fusion(f32[48,128,128]{2,0,1:T(8,128)S(1)} %copy-done.1, f32[128,128,128]{2,1,0:T(8,128)S(1)} %fusion.90, pred[]{:T(512)S(6)} %compare.6, s32[128]{0:T(128)S(1)} %get-tuple-element.214), kind=kOutput, calls=%fused_computation.11.clone.1 | convolution fusion | flops 1209538560 | bytes 14680577 | tf_op jit(solution)/shard_map/while/body/eval_jaxpr/tc,tij->cij/dot_general | solution.py:39
  133.0 0.0 copy-start.2
  133.0 1.6 copy-done.2
  155.5 0.0 collective-permute-done.1
  155.5 1.5 collective-permute-done
  157.0 108.9 %while.23 = (s32[]{:T(128)}, f32[48,128,128]{2,0,1:T(8,128)S(1)}, s32[2,3,128]{2,0,1:T(2,128)S(1)}, f32[192,128,128]{2,1,0:T(8,128)}, f32[16,128,128]{2,1,0:T(8,128)}, /*index=5*/s32[]{:T(128)}, s32[]{:T(128)}, s32[]{}, s32[]{}) while((s32[]{:T(128)}, f32[48,128,128]{2,0,1:T(8,128)S(1)}, s32[2,3,128]{2,0,1:T(2,128)S(1)}, ...), condition=%wide.region_3.4_spmd.clone, body=%wide.region_2.3_spmd.clone.sunk | while | flops 9665282048 | bytes 70259344 | solution.py:59
  157.0 4.7 %fusion.100 = f32[128,128,128]{2,0,1:T(8,128)S(1)} fusion(s32[128]{0:T(128)S(1)} %get-tuple-element.220, f32[2,8,128,128]{3,2,1,0:T(8,128)} %bitcast.154), kind=kOutput, calls=%fused_computation.42.clone.1 | convolution fusion | flops 402655232 | bytes 9437696 | tf_op jit(solution)/shard_map/while/body/eval_jaxpr/dot_general | solution.py:22
  161.8 18.5 %fusion.101 = f32[128,128,128]{2,0,1:T(8,128)} fusion(s32[128]{0:T(128)S(1)} %get-tuple-element.221, f32[24,8,128,128]{3,2,1,0:T(8,128)} %bitcast.155), kind=kOutput, calls=%fused_computation.32.clone.1 | convolution fusion | flops 4831862784 | bytes 20972032 | tf_op jit(solution)/shard_map/while/body/eval_jaxpr/dot_general | solution.py:22
  180.3 21.8 %fusion.102 = f32[128,128,128]{2,1,0:T(8,128)S(1)} fusion(f32[128,128,128]{2,0,1:T(8,128)S(1)} %fusion.100, f32[128,128,128]{2,0,1:T(8,128)} %fusion.101), kind=kOutput, calls=%fused_computation.37.clone.1 | convolution fusion | flops 3221225472 | bytes 25165824 | tf_op jit(solution)/shard_map/while/body/eval_jaxpr/tik,tkj->tij/dot_general | solution.py:31
  202.1 9.4 %select_add_fusion.5 = f32[48,128,128]{2,0,1:T(8,128)S(1)} fusion(f32[48,128,128]{2,0,1:T(8,128)S(1)} %get-tuple-element.233, f32[128,128,128]{2,1,0:T(8,128)S(1)} %fusion.102, pred[]{:T(512)S(6)} %compare.7, s32[128]{0:T(128)S(1)} %get-tuple-element.222), kind=kOutput, calls=%fused_computation.40.clone.1 | convolution fusion | flops 1209538560 | bytes 14680577 | tf_op jit(solution)/shard_map/while/body/eval_jaxpr/tc,tij->cij/dot_general | solution.py:39
  211.5 4.7 %fusion.100 = f32[128,128,128]{2,0,1:T(8,128)S(1)} fusion(s32[128]{0:T(128)S(1)} %get-tuple-element.220, f32[2,8,128,128]{3,2,1,0:T(8,128)} %bitcast.154), kind=kOutput, calls=%fused_computation.42.clone.1 | convolution fusion | flops 402655232 | bytes 9437696 | tf_op jit(solution)/shard_map/while/body/eval_jaxpr/dot_general | solution.py:22
  216.2 18.5 %fusion.101 = f32[128,128,128]{2,0,1:T(8,128)} fusion(s32[128]{0:T(128)S(1)} %get-tuple-element.221, f32[24,8,128,128]{3,2,1,0:T(8,128)} %bitcast.155), kind=kOutput, calls=%fused_computation.32.clone.1 | convolution fusion | flops 4831862784 | bytes 20972032 | tf_op jit(solution)/shard_map/while/body/eval_jaxpr/dot_general | solution.py:22
  234.8 21.8 %fusion.102 = f32[128,128,128]{2,1,0:T(8,128)S(1)} fusion(f32[128,128,128]{2,0,1:T(8,128)S(1)} %fusion.100, f32[128,128,128]{2,0,1:T(8,128)} %fusion.101), kind=kOutput, calls=%fused_computation.37.clone.1 | convolution fusion | flops 3221225472 | bytes 25165824 | tf_op jit(solution)/shard_map/while/body/eval_jaxpr/tik,tkj->tij/dot_general | solution.py:31
  256.6 9.4 %select_add_fusion.5 = f32[48,128,128]{2,0,1:T(8,128)S(1)} fusion(f32[48,128,128]{2,0,1:T(8,128)S(1)} %get-tuple-element.233, f32[128,128,128]{2,1,0:T(8,128)S(1)} %fusion.102, pred[]{:T(512)S(6)} %compare.7, s32[128]{0:T(128)S(1)} %get-tuple-element.222), kind=kOutput, calls=%fused_computation.40.clone.1 | convolution fusion | flops 1209538560 | bytes 14680577 | tf_op jit(solution)/shard_map/while/body/eval_jaxpr/tc,tij->cij/dot_general | solution.py:39
  265.9 5.3 %copy_add_fusion = f32[48,128,128]{2,1,0:T(8,128)} fusion(f32[48,128,128]{2,0,1:T(8,128)S(1)} %get-tuple-element.70, f32[48,128,128]{2,0,1:T(8,128)} %get-tuple-element.69), kind=kLoop, calls=%fused_computation.61 | loop fusion | flops 786432 | bytes 9437184 | tf_op jit(solution)/shard_map/add | solution.py:72
  271.3 0.0 reduce-scatter.2.cloned.1.call-update
  271.3 69.9 %reduce-scatter.2.cloned.1.call-done = f32[12,128,128]{2,1,0:T(8,128)} async-done(((f32[48,128,128]{2,1,0:T(8,128)}), f32[12,128,128]{2,1,0:T(8,128)}) %reduce-scatter.2.cloned.1.call-update) | async-done | bytes 786448 | tf_op jit(solution)/shard_map/reduce_scatter | solution.py:72
  (8 shorter events, 0.0 us)
Async XLA Ops:
  6.5 334.7 %reduce-scatter.2.cloned.1.call-start = ((), (), s32[]{:S(2)}) async-start(), calls=%async_computation.1 | async-start | bytes 3932160 | tf_op jit(solution)/shard_map/reduce_scatter | solution.py:72
  7.2 13.6 %copy-start.5 = (s32[1,1,1,16]{3,2,1,0:T(1,128)S(1)}, s32[1,1,1,16]{3,2,1,0:T(1,128)}, u32[]{:S(2)}) copy-start(s32[1,1,1,16]{3,2,1,0:T(1,128)} %param.12) | copy-start | bytes 196
  7.2 13.6 %copy-start.3 = (f32[1,1,1,16,128,128]{5,4,3,2,1,0:T(8,128)S(1)}, f32[1,1,1,16,128,128]{5,4,3,2,1,0:T(8,128)}, u32[]{:S(2)}) copy-start(f32[1,1,1,16,128,128]{5,4,3,2,1,0:T(8,128)} %param.10) | copy-start | bytes 3145732
  7.2 15.2 %copy-start.4 = (s32[1,1,1,2,3,256]{5,3,4,2,1,0:T(2,128)S(1)}, s32[1,1,1,2,3,256]{5,3,4,2,1,0:T(2,128)}, u32[]{:S(2)}) copy-start(s32[1,1,1,2,3,256]{5,3,4,2,1,0:T(2,128)} %param.13) | copy-start | bytes 18436
  17.2 139.8 %collective-permute-start = (f32[192,128,128]{2,1,0:T(8,128)}, f32[192,128,128]{2,1,0:T(8,128)}, u32[]{:S(2)}, u32[]{:S(2)}) collective-permute-start(f32[192,128,128]{2,1,0:T(8,128)} %bitcast_multiply_fusion), channel_id=1, source_target_pairs={{0,240},{16,0},{32,16},{48,32},{64,48},{80,64},{96,80},{112,96},{1... | collective-permute-start | bytes 37748744 | tf_op jit(solution)/shard_map/ppermute | solution.py:14
  21.9 133.6 %collective-permute-start.1 = (f32[16,128,128]{2,1,0:T(8,128)}, f32[16,128,128]{2,1,0:T(8,128)}, u32[]{:S(2)}, u32[]{:S(2)}) collective-permute-start(f32[16,128,128]{2,1,0:T(8,128)} %bitcast_multiply_fusion.1), channel_id=1, source_target_pairs={{0,12},{4,0},{8,4},{12,8},{1,13},{5,1},{9,5},{13,9},{2,14},{6,2},{... | collective-permute-start | bytes 3145736 | tf_op jit(solution)/shard_map/ppermute | solution.py:14
  22.6 4.9 %copy-start = (f32[192,128,128]{2,1,0:T(8,128)S(1)}, f32[192,128,128]{2,1,0:T(8,128)}, u32[]{:S(2)}) copy-start(f32[192,128,128]{2,1,0:T(8,128)} %get-tuple-element.271) | copy-start | bytes 37748740 | tf_op jit(solution)/shard_map/while
  45.6 22.0 %copy-start.1 = (f32[48,128,128]{2,0,1:T(8,128)S(1)}, f32[48,128,128]{2,0,1:T(8,128)}, u32[]{:S(2)}) copy-start(f32[48,128,128]{2,0,1:T(8,128)} %get-tuple-element.260) | copy-start | bytes 9437188 | tf_op jit(solution)/shard_map/while
  77.0 1.6 copy-start.2
  78.6 4.9 %copy-start = (f32[192,128,128]{2,1,0:T(8,128)S(1)}, f32[192,128,128]{2,1,0:T(8,128)}, u32[]{:S(2)}) copy-start(f32[192,128,128]{2,1,0:T(8,128)} %get-tuple-element.271) | copy-start | bytes 37748740 | tf_op jit(solution)/shard_map/while
  101.6 22.0 %copy-start.1 = (f32[48,128,128]{2,0,1:T(8,128)S(1)}, f32[48,128,128]{2,0,1:T(8,128)}, u32[]{:S(2)}) copy-start(f32[48,128,128]{2,0,1:T(8,128)} %get-tuple-element.260) | copy-start | bytes 9437188 | tf_op jit(solution)/shard_map/while
  133.0 1.6 copy-start.2
Sparse Core Ops, SparseCore 0:
  271.4 69.7 reduce-scatter.1
where the time goes:
time: 352 us; the launch traced here: 348 us
  matrix products  217 us (62%)
  waiting for transfers between devices  71.4 us (20%)
  loops' own time  21.3 us (6%)
  other arithmetic  17.2 us (5%)
  between operations  13.6 us (4%)
  starting transfers between devices  4 us (1%)
    dot_general x8, matrix products, select_blocks(): jnp.dot(chooser, flat, precision=lax.Precision.HIGHEST, preferred_element...  92.5 us
    dot_general x4, matrix products, group_products(): jnp.einsum('tik,tkj->tij', left_blocks, right_blocks, precision=lax.Preci...  87.5 us
    reduce_scatter x1, waiting for transfers between devices, shards(): lax.psum_scatter(first + second, 'rep', scatter_dimension=0, tiled=True)  69.9 us
    dot_general x4, matrix products, group_products(): jnp.einsum('tc,tij->cij', placing, block_products, precision=lax.Precisio...  37.5 us
    another operation x2, loops' own time, batch_products(): totals, _ = lax.scan(advance, initial, groups)  21.3 us
    mul x1, other arithmetic, shards(): a_values[0, 0, 0] * a_live[0, 0, 0][:, None, None].astype(jnp.float32)  10 us
  transfers between devices with their start and end apart: 3, of which 2 were waited for; matrix products, arithmetic and copies ran while one was open for 32% of the time, Pallas kernels for 0%

commit v1 on v0

v1 whole, which is shorter than its diff:
```python
import jax
import jax.numpy as jnp
from jax import lax
from jax.experimental import pallas as pl
from jax.experimental.pallas import tpu as pltpu
from jax.sharding import PartitionSpec as P

BS = 128
C_SLOTS = 48
B_KEEP = 8
BATCH = 256
UNROLL = 8
f32 = jnp.float32
bf16 = jnp.bfloat16


def pack_kernel(live_ref, b_ref, out_ref, which, sems):
    for k in range(B_KEEP):
        which[k] = 0
    def find(r, n):
        which[n] = jnp.where(live_ref[r] > 0, r, 0)
        return n + live_ref[r]
    lax.fori_loop(0, live_ref.shape[0], find, 0, unroll=True)
    copies = [pltpu.make_async_copy(b_ref.at[which[k]], out_ref.at[k], sems.at[k]) for k in range(B_KEEP)]
    for c in copies: c.start()
    for c in copies: c.wait()

def pack_right(b, live):
    return pl.pallas_call(
        pack_kernel,
        out_shape=jax.ShapeDtypeStruct((B_KEEP, BS, BS), f32),
        in_specs=[pl.BlockSpec(memory_space=pltpu.SMEM), pl.BlockSpec(memory_space=pl.ANY)],
        out_specs=pl.BlockSpec(memory_space=pltpu.VMEM),
        scratch_shapes=[pltpu.SMEM((B_KEEP + 1,), jnp.int32), pltpu.SemaphoreType.DMA((B_KEEP,))],
        name="pack_right",
    )(live, b)

def product_kernel(table_ref, a_live_ref, b_live_ref, a_ref, b_ref, out_ref,
                   total, blocks, weights, rank, left_list, right_list, target_list, sems, out_sem):
    def count(r, n):
        rank[r] = n
        return n + b_live_ref[r]
    lax.fori_loop(0, b_live_ref.shape[0], count, 0, unroll=True)

    def keep(t, n):
        l = table_ref[0, t]; r = table_ref[1, t]; c = table_ref[2, t]
        left_list[n] = l
        right_list[n] = rank[r]
        target_list[n] = c
        useful = a_live_ref[l] * b_live_ref[r]
        return n + jnp.where(c < C_SLOTS, useful, 0)
    n = lax.fori_loop(0, BATCH, keep, 0, unroll=8)
    for u in range(UNROLL):
        left_list[n + u] = 0
        right_list[n + u] = 0
        target_list[n + u] = C_SLOTS
    groups = (n + UNROLL - 1) // UNROLL

    def fetch(g, _):
        for u in range(UNROLL):
            t = g * UNROLL + u
            pltpu.make_async_copy(a_ref.at[left_list[t]], blocks.at[t], sems.at[g]).start()
        return 0
    lax.fori_loop(0, groups, fetch, 0)

    for k in range(B_KEEP):
        b = b_ref[k]
        hi = b.astype(bf16)
        lo = (b - hi.astype(f32)).astype(bf16)
        weights[k, :BS, :BS] = hi
        weights[k, :BS, BS:] = lo
        weights[k, BS:, :BS] = hi
        weights[k, BS:, BS:] = jnp.zeros_like(lo)

    def clear(c, _):
        total[c] = jnp.zeros((BS, BS), f32)
        return 0
    lax.fori_loop(0, C_SLOTS, clear, 0, unroll=4)

    def work(g, _):
        here = pl.ds(g * UNROLL, UNROLL)
        pltpu.make_async_copy(a_ref.at[pl.ds(0, UNROLL)], blocks.at[here], sems.at[g]).wait()
        products = []
        for u in range(UNROLL):
            t = g * UNROLL + u
            a = blocks[t]
            hi = a.astype(bf16)
            lo = (a - hi.astype(f32)).astype(bf16)
            both = jnp.dot(jnp.concatenate([hi, lo], axis=1), weights[right_list[t]], preferred_element_type=f32)
            products.append(both[:, :BS] + both[:, BS:])
        for u in range(UNROLL):
            c = target_list[g * UNROLL + u]
            total[c] = total[c] + products[u]
        return 0
    lax.fori_loop(0, groups, work, 0)
    out = pltpu.make_async_copy(total.at[pl.ds(0, C_SLOTS)], out_ref, out_sem)
    out.start(); out.wait()

def products(a, a_live, b_kept, b_live, table, name):
    most = BATCH + UNROLL
    return pl.pallas_call(
        product_kernel,
        out_shape=jax.ShapeDtypeStruct((C_SLOTS, BS, BS), f32),
        in_specs=[pl.BlockSpec(memory_space=pltpu.SMEM)] * 3
        + [pl.BlockSpec(memory_space=pl.ANY), pl.BlockSpec(memory_space=pltpu.VMEM)],
        out_specs=pl.BlockSpec(memory_space=pl.ANY),
        scratch_shapes=[
            pltpu.VMEM((C_SLOTS + 1, BS, BS), f32),
            pltpu.VMEM((most, BS, BS), f32),
            pltpu.VMEM((B_KEEP, 2 * BS, 2 * BS), bf16),
            pltpu.SMEM((b_live.shape[0],), jnp.int32),
            pltpu.SMEM((most,), jnp.int32), pltpu.SMEM((most,), jnp.int32), pltpu.SMEM((most,), jnp.int32),
            pltpu.SemaphoreType.DMA((most // UNROLL,)),
            pltpu.SemaphoreType.DMA,
        ],
        compiler_params=pltpu.CompilerParams(vmem_limit_bytes=40 * 2**20),
        name=name,
    )(table, a_live, b_live, a, b_kept)


def shards(a_values, b_values, a_live, b_live, triples):
    a, a_on = a_values[0, 0, 0], a_live[0, 0, 0]
    b, b_on = b_values[0, 0, 0], b_live[0, 0, 0]
    tables = triples[0, 0, 0]
    rows, cols = lax.axis_size("row"), lax.axis_size("col")
    to_left = [(i * cols + (j + 1) % cols, (i + 1) % rows * cols + j) for i in range(rows) for j in range(cols)]
    down = [(i, (i + 1) % rows) for i in range(rows)]
    up = [(i, (i - 1) % rows) for i in range(rows)]
    kept = pack_right(b, b_on)
    kept_far = lax.ppermute(kept, ("row", "col"), to_left)
    b_on_far = lax.ppermute(b_on, ("row", "col"), to_left)
    table_far = lax.ppermute(tables[1], "row", down)
    second = products(a, a_on, kept_far, b_on_far, table_far, "second")
    first = products(a, a_on, kept, b_on, tables[0], "first")
    second = lax.ppermute(second, "row", up)
    shares = lax.psum_scatter(first + second, "rep", scatter_dimension=0, tiled=True)
    return shares.reshape(1, 1, C_SLOTS // lax.axis_size("rep"), BS, BS)


def solution(mesh):
    placed = (
        P("row", "col", "rep", None, None, None),
        P("row", "col", "rep", None, None, None),
        P("row", "col", "rep", None),
        P("row", "col", "rep", None),
        P("row", "col", "rep", None, None, None),
    )
    return jax.shard_map(
        shards,
        mesh=mesh,
        in_specs=placed,
        out_specs=P("row", "col", "rep", None, None),
        check_vma=False,
    )
```

time: 352 us -> 149 us (0.42)
  matrix products: 217 us -> 0 us
  waiting for transfers between devices: 71.4 us -> 107 us
  loops' own time: 21.3 us -> 0 us
  other arithmetic: 17.2 us -> 2.13 us
  Pallas kernels: 0 us -> 12.8 us
  starting transfers between devices: 4 us -> 11 us
    dot_general x16 -> x0, matrix products: 217 us -> none  [the longest x8 92.5 us: select_blocks(): jnp.dot(chooser, flat, precision=lax.Precision.HIGHEST, preferred_element...]
    ppermute x2 -> x4, waiting for transfers between devices: 1.48 us -> 36.5 us  [the longest x1 29.3 us: shards(): second = lax.ppermute(second, 'row', up)]
    another operation x2 -> x0, loops' own time: 21.3 us -> none  [batch_products(): totals, _ = lax.scan(advance, initial, groups)]
    pallas_call x0 -> x3, Pallas kernels: none -> 12.8 us  [the longest x2 10.2 us: products(): pl.pallas_call(product_kernel, out_shape=jax.ShapeDtypeStruct((C_SLOTS, B...]
    mul x2 -> x0, other arithmetic: 11.1 us -> none  [the longest x1 10 us: shards(): a_values[0, 0, 0] * a_live[0, 0, 0][:, None, None].astype(jnp.float32)]
    ppermute x2 -> x4, starting transfers between devices: 4 us -> 11 us  [the longest x1 6.26 us: shards(): second = lax.ppermute(second, 'row', up)]
  transfers between devices with their start and end apart: 3 -> 5, of which waited for: 2 -> 3; matrix products, arithmetic and copies ran while one was open for 32% -> 1% of each run, Pallas kernels for 0% -> 4%
where the time goes in v1:
time: 149 us; the launch traced here: 148 us
  waiting for transfers between devices  107 us (72%)
  between operations  13.4 us (9%)
  Pallas kernels  12.8 us (9%)
  starting transfers between devices  11 us (7%)
  other arithmetic  2.13 us (1%)
    reduce_scatter x1, waiting for transfers between devices, shards(): lax.psum_scatter(first + second, 'rep', scatter_dimension=0, tiled=True)  70.8 us
    ppermute x1, waiting for transfers between devices, shards(): second = lax.ppermute(second, 'row', up)  29.3 us
    pallas_call x2, Pallas kernels, products(): pl.pallas_call(product_kernel, out_shape=jax.ShapeDtypeStruct((C_SLOTS, B...  10.2 us
    ppermute x1, waiting for transfers between devices, shards(): b_on_far = lax.ppermute(b_on, ('row', 'col'), to_left)  7.16 us
    ppermute x1, starting transfers between devices, shards(): second = lax.ppermute(second, 'row', up)  6.26 us
  transfers between devices with their start and end apart: 5, of which 3 were waited for; matrix products, arithmetic and copies ran while one was open for 1% of the time, Pallas kernels for 4%

profile of v1, /device:TPU:8, one launch (start us, length us, event | category | flops | bytes accessed | tf_op | source)
XLA Modules:
  0.0 148.2 jit_solution(8537484695789088492)
XLA Ops:
  6.5 0.0 reduce-scatter.2.cloned.1.call-start
  6.5 2.6 %pack_right.1.b_ref = f32[8,128,128]{2,1,0:T(8,128)} custom-call(s32[16]{0:T(128)} %bitcast.14, f32[16,128,128]{2,1,0:T(8,128)} %bitcast.19), custom_call_target="tpu_custom_call" | custom-call | tf_op jit(solution)/shard_map/pack_right/pallas_call | solution.py:29
  9.2 0.1 collective-permute-start.2
  9.3 0.8 fusion
  10.0 2.0 %collective-permute-start = (s32[3,256]{1,0:T(4,128)S(1)}, s32[3,256]{1,0:T(4,128)S(1)}, u32[]{:S(2)}, u32[]{:S(2)}) collective-permute-start(s32[3,256]{1,0:T(4,128)S(1)} %bitcast.20), channel_id=1, source_target_pairs={{0,16},{16,32},{32,48},{48,64},{64,80},{80,96},{96,112},{112,128},... | collective-permute-start | bytes 9224 | tf_op jit(solution)/shard_map/ppermute | solution.py:132
  12.0 2.7 %collective-permute-start.1 = (s32[16]{0:T(128)}, s32[16]{0:T(128)S(1)}, u32[]{:S(2)}, u32[]{:S(2)}) collective-permute-start(s32[16]{0:T(128)} %bitcast.15), channel_id=1, source_target_pairs={{4,16},{8,20},{12,24},{0,28},{20,32},{24,36},{28,40},{16,44},{36,4... | collective-permute-start | bytes 200 | tf_op jit(solution)/shard_map/ppermute | solution.py:131
  14.7 7.2 %collective-permute-done.1.b_live_ref = s32[16]{0:T(128)S(1)} collective-permute-done((s32[16]{0:T(128)}, s32[16]{0:T(128)S(1)}, u32[]{:S(2)}, u32[]{:S(2)}) %collective-permute-start.1) | collective-permute-done | bytes 96 | tf_op jit(solution)/shard_map/ppermute | solution.py:131
  21.9 0.0 collective-permute-done.table_ref
  21.9 0.0 collective-permute-done.2.b_ref
  21.9 0.0 copy-start.1
  21.9 0.7 copy-done.1
  22.6 0.0 copy-start
  22.6 0.0 copy-start.2
  22.6 0.0 copy-start.3
  22.6 4.8 %second.1 = f32[48,128,128]{2,1,0:T(8,128)S(1)} custom-call(s32[3,256]{1,0:T(4,128)S(1)} %collective-permute-done.table_ref, s32[192]{0:T(256)S(1)} %bitcast.12, s32[16]{0:T(128)S(1)} %collective-permute-done.1.b_live_ref, f32[192,128,128]{2,1,0:T(8,128)} %bitcast.17, f32[8,128,128]{2,1,0:T(8,128)S(1)} %collective-permute-done.2.b_ref), custom_call_target="tpu_custom_call" | custom-call | tf_op jit(solution)/shard_map/second/pallas_call | solution.py:101
  27.4 6.3 %collective-permute-start.3 = (f32[48,128,128]{2,1,0:T(8,128)S(1)}, f32[48,128,128]{2,1,0:T(8,128)S(1)}, u32[]{:S(2)}, u32[]{:S(2)}) collective-permute-start(f32[48,128,128]{2,1,0:T(8,128)S(1)} %second.1), channel_id=1, source_target_pairs={{0,240},{16,0},{32,16},{48,32},{64,48},{80,64},{96,80},{112,96},{1... | collective-permute-start | bytes 9437192 | tf_op jit(solution)/shard_map/ppermute | solution.py:135
  33.6 0.0 copy-done
  33.6 0.0 copy-done.2
  33.6 0.0 copy-done.3
  33.6 5.4 %first.1 = f32[48,128,128]{2,1,0:T(8,128)S(1)} custom-call(s32[3,256]{1,0:T(4,128)S(1)} %bitcast.11, s32[192]{0:T(256)S(1)} %bitcast.13, s32[16]{0:T(128)S(1)} %bitcast.16, f32[192,128,128]{2,1,0:T(8,128)} %bitcast.18, f32[8,128,128]{2,1,0:T(8,128)S(1)} %copy-done), custom_call_target="tpu_custom_call" | custom-call | tf_op jit(solution)/shard_map/first/pallas_call | solution.py:101
  39.1 29.3 %collective-permute-done.3 = f32[48,128,128]{2,1,0:T(8,128)S(1)} collective-permute-done((f32[48,128,128]{2,1,0:T(8,128)S(1)}, f32[48,128,128]{2,1,0:T(8,128)S(1)}, u32[]{:S(2)}, u32[]{:S(2)}) %collective-permute-start.3) | collective-permute-done | bytes 3145760 | tf_op jit(solution)/shard_map/ppermute | solution.py:135
  68.4 2.1 %add.5 = f32[48,128,128]{2,1,0:T(8,128)} add(f32[48,128,128]{2,1,0:T(8,128)S(1)} %first.1, f32[48,128,128]{2,1,0:T(8,128)S(1)} %collective-permute-done.3) | non-fusion elementwise | flops 786432 | bytes 9437184 | tf_op jit(solution)/shard_map/add | solution.py:136
  70.5 0.0 reduce-scatter.2.cloned.1.call-update
  70.6 70.8 %reduce-scatter.2.cloned.1.call-done = f32[12,128,128]{2,1,0:T(8,128)} async-done(((f32[48,128,128]{2,1,0:T(8,128)}), f32[12,128,128]{2,1,0:T(8,128)}) %reduce-scatter.2.cloned.1.call-update) | async-done | bytes 786448 | tf_op jit(solution)/shard_map/reduce_scatter | solution.py:136
  (2 shorter events, 0.0 us)
Async XLA Ops:
  6.5 134.8 %reduce-scatter.2.cloned.1.call-start = ((), (), s32[]{:S(2)}) async-start(), calls=%async_computation.1 | async-start | bytes 3932160 | tf_op jit(solution)/shard_map/reduce_scatter | solution.py:136
  9.2 12.7 %collective-permute-start.2 = (f32[8,128,128]{2,1,0:T(8,128)}, f32[8,128,128]{2,1,0:T(8,128)S(1)}, u32[]{:S(2)}, u32[]{:S(2)}) collective-permute-start(f32[8,128,128]{2,1,0:T(8,128)} %pack_right.1.b_ref), channel_id=1, source_target_pairs={{4,16},{8,20},{12,24},{0,28},{20,32},{24,36},{28,40},{16,44},{36,4... | collective-permute-start | bytes 1572872 | tf_op jit(solution)/shard_map/ppermute | solution.py:130
  10.0 11.9 %collective-permute-start = (s32[3,256]{1,0:T(4,128)S(1)}, s32[3,256]{1,0:T(4,128)S(1)}, u32[]{:S(2)}, u32[]{:S(2)}) collective-permute-start(s32[3,256]{1,0:T(4,128)S(1)} %bitcast.20), channel_id=1, source_target_pairs={{0,16},{16,32},{32,48},{48,64},{64,80},{80,96},{96,112},{112,128},... | collective-permute-start | bytes 9224 | tf_op jit(solution)/shard_map/ppermute | solution.py:132
  12.0 9.9 %collective-permute-start.1 = (s32[16]{0:T(128)}, s32[16]{0:T(128)S(1)}, u32[]{:S(2)}, u32[]{:S(2)}) collective-permute-start(s32[16]{0:T(128)} %bitcast.15), channel_id=1, source_target_pairs={{4,16},{8,20},{12,24},{0,28},{20,32},{24,36},{28,40},{16,44},{36,4... | collective-permute-start | bytes 200 | tf_op jit(solution)/shard_map/ppermute | solution.py:131
  21.9 0.7 copy-start.1
  22.6 11.1 %copy-start = (f32[8,128,128]{2,1,0:T(8,128)S(1)}, f32[8,128,128]{2,1,0:T(8,128)}, u32[]{:S(2)}) copy-start(f32[8,128,128]{2,1,0:T(8,128)} %pack_right.1.b_ref) | copy-start | bytes 1572868
  22.6 11.1 %copy-start.2 = (s32[1,1,1,192]{3,2,1,0:T(1,128)S(1)}, s32[1,1,1,192]{3,2,1,0:T(1,128)}, u32[]{:S(2)}) copy-start(s32[1,1,1,192]{3,2,1,0:T(1,128)} %param.7) | copy-start | bytes 2308
  22.6 11.1 %copy-start.3 = (s32[1,1,1,16]{3,2,1,0:T(1,128)S(1)}, s32[1,1,1,16]{3,2,1,0:T(1,128)}, u32[]{:S(2)}) copy-start(s32[1,1,1,16]{3,2,1,0:T(1,128)} %param.8) | copy-start | bytes 196
  27.4 41.0 %collective-permute-start.3 = (f32[48,128,128]{2,1,0:T(8,128)S(1)}, f32[48,128,128]{2,1,0:T(8,128)S(1)}, u32[]{:S(2)}, u32[]{:S(2)}) collective-permute-start(f32[48,128,128]{2,1,0:T(8,128)S(1)} %second.1), channel_id=1, source_target_pairs={{0,240},{16,0},{32,16},{48,32},{64,48},{80,64},{96,80},{112,96},{1... | collective-permute-start | bytes 9437192 | tf_op jit(solution)/shard_map/ppermute | solution.py:135
Sparse Core Ops, SparseCore 0:
  70.7 70.6 reduce-scatter.1

commit v2 on v1

v2 whole, which is shorter than its diff:
```python
import jax
import jax.numpy as jnp
from jax import lax
from jax.experimental import pallas as pl
from jax.experimental.pallas import tpu as pltpu
from jax.sharding import PartitionSpec as P

BS = 128
C_SLOTS = 48
B_KEEP = 8
BATCH = 256
UNROLL = 16
N_ROW = 16
N_REP = 4
SHARE = C_SLOTS // N_REP
HALF = SHARE // 2
f32 = jnp.float32
bf16 = jnp.bfloat16


def pack_kernel(live_ref, b_ref, out_ref, which, sems):
    for k in range(B_KEEP):
        which[k] = 0

    def find(r, n):
        which[n] = jnp.where(live_ref[r] > 0, r, 0)
        return n + live_ref[r]

    lax.fori_loop(0, live_ref.shape[0], find, 0, unroll=True)
    copies = [pltpu.make_async_copy(b_ref.at[which[k]], out_ref.at[k], sems.at[k]) for k in range(B_KEEP)]
    for c in copies:
        c.start()
    for c in copies:
        c.wait()


def pack_right(b, live):
    return pl.pallas_call(
        pack_kernel,
        out_shape=jax.ShapeDtypeStruct((B_KEEP, BS, BS), f32),
        in_specs=[pl.BlockSpec(memory_space=pltpu.SMEM), pl.BlockSpec(memory_space=pl.ANY)],
        out_specs=pl.BlockSpec(memory_space=pltpu.VMEM),
        scratch_shapes=[pltpu.SMEM((B_KEEP + 1,), jnp.int32), pltpu.SemaphoreType.DMA((B_KEEP,))],
        name="pack_right",
    )(live, b)


def product_kernel(extra, parts, far, table_ref, a_live_ref, b_live_ref, a_ref, b_ref, *rest):
    rest = rest[extra:]
    outs = rest[: len(parts)]
    total, weights, rank, moved, left_list, right_list, target_list, out_sems = rest[len(parts):]

    def count(r, n):
        rank[r] = n
        return n + b_live_ref[r]

    lax.fori_loop(0, b_live_ref.shape[0], count, 0, unroll=True)

    layer = lax.axis_index("rep")
    if far:
        row = lax.axis_index("row")
        layer = layer + jnp.where(lax.rem(row, 4) == 2, 1, 0)
    for place, ahead in enumerate((2, 3, 1, 0)):
        owner = lax.rem(layer + ahead, N_REP)
        moved[owner] = (place - owner) * SHARE
    moved[N_REP] = 0

    def keep(t, n):
        l = table_ref[0, t]
        r = table_ref[1, t]
        c = table_ref[2, t]
        left_list[n] = l
        right_list[n] = rank[r]
        target_list[n] = c + moved[(c * 43) >> 9]
        return n + jnp.where(c < C_SLOTS, a_live_ref[l] * b_live_ref[r], 0)

    n = lax.fori_loop(0, BATCH, keep, 0, unroll=8)
    for u in range(UNROLL):
        left_list[n + u] = 0
        right_list[n + u] = 0
        target_list[n + u] = C_SLOTS
    groups = (n + UNROLL - 1) // UNROLL
    for k in range(B_KEEP):
        b = b_ref[k]
        hi = b.astype(bf16)
        lo = (b - hi.astype(f32)).astype(bf16)
        weights[k, :BS, :BS] = hi
        weights[k, :BS, BS:] = lo
        weights[k, BS:, :BS] = hi
        weights[k, BS:, BS:] = jnp.zeros_like(lo)

    def clear(c, _):
        total[c] = jnp.zeros((BS, BS), f32)
        return 0

    lax.fori_loop(0, C_SLOTS, clear, 0, unroll=4)

    def work(g, _):
        for u in range(UNROLL):
            t = g * UNROLL + u
            a = a_ref[left_list[t]]
            hi = a.astype(bf16)
            lo = (a - hi.astype(f32)).astype(bf16)
            both = jnp.dot(
                jnp.concatenate([hi, lo], axis=1), weights[right_list[t]], preferred_element_type=f32
            )
            c = target_list[t]
            total[c] = total[c] + (both[:, :BS] + both[:, BS:])
        return 0

    lax.fori_loop(0, groups, work, 0)
    copies = [
        pltpu.make_async_copy(total.at[pl.ds(at, size)], outs[k], out_sems.at[k]) for k, (at, size) in enumerate(parts)
    ]
    for c in copies:
        c.start()
    for c in copies:
        c.wait()


def products(a, a_live, b_kept, b_live, table, first, parts, far, name):
    most = BATCH + UNROLL

    def kernel(*refs):
        product_kernel(len(first), parts, far, *refs)

    return pl.pallas_call(
        kernel,
        out_shape=[jax.ShapeDtypeStruct((size, BS, BS), f32) for _, size in parts],
        in_specs=[pl.BlockSpec(memory_space=pltpu.SMEM)] * 3
        + [pl.BlockSpec(memory_space=pltpu.VMEM)] * 2
        + [pl.BlockSpec(memory_space=pl.ANY)] * len(first),
        out_specs=[pl.BlockSpec(memory_space=pl.ANY)] * len(parts),
        scratch_shapes=[
            pltpu.VMEM((C_SLOTS + 1, BS, BS), f32),
            pltpu.VMEM((B_KEEP, 2 * BS, 2 * BS), bf16),
            pltpu.SMEM((b_live.shape[0],), jnp.int32),
            pltpu.SMEM((N_REP + 1,), jnp.int32),
            pltpu.SMEM((most,), jnp.int32),
            pltpu.SMEM((most,), jnp.int32),
            pltpu.SMEM((most,), jnp.int32),
            pltpu.SemaphoreType.DMA((len(parts),)),
        ],
        compiler_params=pltpu.CompilerParams(vmem_limit_bytes=26 * 2**20),
        name=name,
    )(table, a_live, b_live, a, b_kept, *first)


def after(x, first, flops=0):
    def kernel(x_ref, first_ref, out_ref):
        pass

    return pl.pallas_call(
        kernel,
        out_shape=jax.ShapeDtypeStruct(x.shape, x.dtype),
        in_specs=[pl.BlockSpec(memory_space=pl.ANY)] * 2,
        out_specs=pl.BlockSpec(memory_space=pl.ANY),
        input_output_aliases={0: 0},
        cost_estimate=pl.CostEstimate(flops=flops, bytes_accessed=0, transcendentals=0),
        name="after",
    )(x, first)


def moves(rule):
    pairs = []
    for x in range(4):
        for z in range(8):
            for core in range(2):
                to = rule(x, z, core)
                if to is not None:
                    ends = [(4 * (u % 4) + 2 * (w % 8 % 2) + c) * N_REP + w % 8 // 2 for u, w, c in ((x, z, core), to)]
                    pairs.append(tuple(ends))
    return pairs


def send(x, rule):
    return lax.ppermute(x, ("row", "rep"), moves(rule))


def to_other_core(x, z, core):
    return (x, z, 0) if core == 1 else None


def to_owner_ring(step):
    def rule(x, z, core):
        if core == 1:
            return None
        return (x if z % 2 == 1 else x - 1, z + step, 1)

    return rule


def layers_on(step, cores):
    def rule(x, z, core):
        return (x, z + 2 * step, core) if core in cores else None

    return rule


def shards(a_values, b_values, a_live, b_live, triples):
    a, a_on = a_values[0, 0, 0], a_live[0, 0, 0]
    b, b_on = b_values[0, 0, 0], b_live[0, 0, 0]
    tables = triples[0, 0, 0]
    rows, cols = lax.axis_size("row"), lax.axis_size("col")
    to_left = [(i * cols + (j + 1) % cols, (i + 1) % rows * cols + j) for i in range(rows) for j in range(cols)]
    next_row = [(i, (i + 1) % rows) for i in range(rows)]
    kept = pack_right(b, b_on)
    kept_far = lax.ppermute(kept, ("row", "col"), to_left)
    b_on_far = lax.ppermute(b_on, ("row", "col"), to_left)
    table_far = lax.ppermute(tables[1], "row", next_row)

    shares_at = [(0, HALF), (HALF, HALF)] + [(k * SHARE, SHARE) for k in range(1, N_REP)]
    own0a, own0b, own_down, own_up, own_here = products(a, a_on, kept, b_on, tables[0], (), shares_at, False, "first")
    shares_at = [(k * SHARE, SHARE) for k in range(N_REP)] + [(SHARE, C_SLOTS - SHARE)]
    far0, far1, far2, far3, rest = products(a, a_on, kept_far, b_on_far, table_far, (own0a,), shares_at, True, "second")
    odd_down = send(far0, to_owner_ring(-1))
    odd_up = send(far2, to_owner_ring(1))
    near0 = send(far0, to_other_core)

    down = own0a + near0[:HALF]
    up = own0b + near0[HALF:]
    near = send(after(rest, down), to_other_core)
    odd_down = after(odd_down, down, 5 * 10**9)
    odd_up = after(odd_up, up, 5 * 10**9)
    down = send(down, layers_on(-1, (0, 1)))
    up = send(up, layers_on(1, (0, 1)))
    late_down = send(after(far1, odd_down), to_owner_ring(-1))
    late_up = send(after(far3, odd_up), to_owner_ring(1))
    nothing = jnp.zeros((HALF, BS, BS), f32)
    down = send(own_down + odd_down + near[:SHARE] + jnp.concatenate([down, nothing]), layers_on(-1, (0, 1)))
    up = send(own_up + odd_up + near[SHARE : 2 * SHARE] + jnp.concatenate([nothing, up]), layers_on(1, (0, 1)))
    shares = own_here + near[2 * SHARE :] + late_down + late_up + down + up
    return shares.reshape(1, 1, SHARE, BS, BS)


def solution(mesh):
    placed = (
        P("row", "col", "rep", None, None, None),
        P("row", "col", "rep", None, None, None),
        P("row", "col", "rep", None),
        P("row", "col", "rep", None),
        P("row", "col", "rep", None, None, None),
    )
    return jax.shard_map(
        shards,
        mesh=mesh,
        in_specs=placed,
        out_specs=P("row", "col", "rep", None, None),
        check_vma=False,
    )
```

time: 149 us -> 119 us (0.80)
  waiting for transfers between devices: 107 us -> 45.6 us
  starting transfers between devices: 11 us -> 44.4 us
  between operations: 13.4 us -> 0.17 us
  local copies, waits for them, and re-layouts: 1.47 us -> 9.18 us
  other arithmetic: 2.13 us -> 6.13 us
    reduce_scatter x1 -> x0, waiting for transfers between devices: 70.8 us -> none  [shards(): lax.psum_scatter(first + second, 'rep', scatter_dimension=0, tiled=True)]
    ppermute x2 -> x11, starting transfers between devices: 8.24 us -> 41.6 us  [the longest x10 39.6 us: send(): return lax.ppermute(x, ('row', 'rep'), moves(rule))]
    ppermute x2 -> x11, waiting for transfers between devices: 29.3 us -> 45.6 us  [the longest x10 45.6 us: send(): return lax.ppermute(x, ('row', 'rep'), moves(rule))]
    unnamed x10 -> x22, local copies, waits for them, and re-layouts: 0.7 us -> 8.4 us
    ppermute x1, waiting for transfers between devices: 7.16 us -> 0.01 us  [shards(): b_on_far = lax.ppermute(b_on, ('row', 'col'), to_left)]
    reshape x0 -> x1, other arithmetic: none -> 2.58 us  [shards(): return shares.reshape(1, 1, SHARE, BS, BS)]
    add x1 -> x2, other arithmetic: 2.13 us -> 3.55 us  [the longest x1 2.55 us: shards(): own_down + odd_down + near[:SHARE] + jnp.concatenate([down, nothing])]
    pallas_call x2 -> x7, Pallas kernels: 10.2 us -> 10 us  [the longest x2 10 us: products(): pl.pallas_call(kernel, out_shape=[jax.ShapeDtypeStruct((size, BS, BS), f3...]
  transfers between devices with their start and end apart: 5 -> 13, of which waited for: 3 -> 7; matrix products, arithmetic and copies ran while one was open for 1% -> 3% of each run, Pallas kernels for 4% -> 4%
where the time goes in v2:
time: 119 us; the launch traced here: 118 us
  waiting for transfers between devices  45.6 us (38%)
  starting transfers between devices  44.4 us (37%)
  Pallas kernels  12.7 us (11%)
  local copies, waits for them, and re-layouts  9.18 us (8%)
  other arithmetic  6.13 us (5%)
    ppermute x10, waiting for transfers between devices, send(): return lax.ppermute(x, ('row', 'rep'), moves(rule))  45.6 us
    ppermute x10, starting transfers between devices, send(): return lax.ppermute(x, ('row', 'rep'), moves(rule))  39.6 us
    pallas_call x2, Pallas kernels, products(): pl.pallas_call(kernel, out_shape=[jax.ShapeDtypeStruct((size, BS, BS), f3...  10 us
    unnamed x22, local copies, waits for them, and re-layouts  8.4 us
    ppermute x1, starting transfers between devices, shards(): b_on_far = lax.ppermute(b_on, ('row', 'col'), to_left)  2.71 us
    pallas_call x1, Pallas kernels, pack_right(): pl.pallas_call(pack_kernel, out_shape=jax.ShapeDtypeStruct((B_KEEP, BS, B...  2.62 us
    reshape x1, other arithmetic, shards(): return shares.reshape(1, 1, SHARE, BS, BS)  2.58 us
    add x1, other arithmetic, shards(): own_down + odd_down + near[:SHARE] + jnp.concatenate([down, nothing])  2.55 us
  transfers between devices with their start and end apart: 13, of which 7 were waited for; matrix products, arithmetic and copies ran while one was open for 3% of the time, Pallas kernels for 4%

profile of v2, /device:TPU:8, one launch (start us, length us, event | category | flops | bytes accessed | tf_op | source)
XLA Modules:
  0.0 118.2 jit_solution(13847967921973896162)
XLA Ops:
  0.0 2.6 %pack_right.1.refs_4_ = f32[8,128,128]{2,1,0:T(8,128)} custom-call(s32[16]{0:T(128)} %bitcast.17, f32[16,128,128]{2,1,0:T(8,128)} %bitcast.20), custom_call_target="tpu_custom_call" | custom-call | tf_op jit(solution)/shard_map/pack_right/pallas_call | solution.py:38
  2.6 0.1 collective-permute-start.2
  2.7 0.8 fusion.7
  3.5 2.0 %collective-permute-start = (s32[3,256]{1,0:T(4,128)S(1)}, s32[3,256]{1,0:T(4,128)S(1)}, u32[]{:S(2)}, u32[]{:S(2)}) collective-permute-start(s32[3,256]{1,0:T(4,128)S(1)} %bitcast.21), channel_id=1, source_target_pairs={{0,16},{16,32},{32,48},{48,64},{64,80},{80,96},{96,112},{112,128},... | collective-permute-start | bytes 9224 | tf_op jit(solution)/shard_map/ppermute | solution.py:210
  5.5 2.7 %collective-permute-start.1 = (s32[16]{0:T(128)}, s32[16]{0:T(128)S(1)}, u32[]{:S(2)}, u32[]{:S(2)}) collective-permute-start(s32[16]{0:T(128)} %bitcast.18), channel_id=1, source_target_pairs={{4,16},{8,20},{12,24},{0,28},{20,32},{24,36},{28,40},{16,44},{36,4... | collective-permute-start | bytes 200 | tf_op jit(solution)/shard_map/ppermute | solution.py:209
  8.2 0.0 copy-start
  8.2 4.6 %copy-done = f32[1,1,1,192,128,128]{5,4,3,2,1,0:T(8,128)S(1)} copy-done((f32[1,1,1,192,128,128]{5,4,3,2,1,0:T(8,128)S(1)}, f32[1,1,1,192,128,128]{5,4,3,2,1,0:T(8,128)}, u32[]{:S(2)}) %copy-start) | copy-done | bytes 12582936
  12.8 0.0 copy-start.3
  12.8 1.0 copy-done.3
  13.8 0.0 copy-start.6
  13.8 0.7 copy-done.6
  14.5 0.0 copy-start.7
  14.5 0.7 copy-done.7
  15.1 0.0 copy-start.1
  15.1 4.7 %first.1 = (f32[6,128,128]{2,1,0:T(8,128)S(1)}, f32[6,128,128]{2,1,0:T(8,128)S(1)}, f32[12,128,128]{2,1,0:T(8,128)S(1)}, f32[12,128,128]{2,1,0:T(8,128)S(1)}, f32[12,128,128]{2,1,0:T(8,128)S(1)}) custom-call(s32[3,256]{1,0:T(4,128)S(1)} %bitcast.14, s32[192]{0:T(256)S(1)} %bitcast.15, s32[16]{0:T(128)S(1)} %bitcast.19, f32[192,128,128]{2,1,0:T(8,128)S(1)} %bitcast.12, ...), custom_call_target="tpu_custom_call" | custom-call | tf_op jit(solution)/shard_map/first/pallas_call | solution.py:127
  19.8 0.0 collective-permute-done.1.refs_2_
  19.8 0.0 collective-permute-done.refs_0_
  19.8 0.0 collective-permute-done.2.refs_4_
  19.8 0.0 copy-done.1
  19.8 5.4 %second.1 = (f32[12,128,128]{2,1,0:T(8,128)S(1)}, f32[12,128,128]{2,1,0:T(8,128)S(1)}, f32[12,128,128]{2,1,0:T(8,128)S(1)}, f32[12,128,128]{2,1,0:T(8,128)S(1)}, f32[36,128,128]{2,1,0:T(8,128)S(1)}) custom-call(s32[3,256]{1,0:T(4,128)S(1)} %collective-permute-done.refs_0_, s32[192]{0:T(256)S(1)} %bitcast.16, s32[16]{0:T(128)S(1)} %collective-permute-done.1.refs_2_, ...), custom_call_target="tpu_custom_call" | custom-call | tf_op jit(solution)/shard_map/second/pallas_call | solution.py:127
  25.2 0.0 copy-start.2
  25.2 1.4 %copy-done.2 = f32[36,128,128]{2,1,0:T(8,128)} copy-done((f32[36,128,128]{2,1,0:T(8,128)}, f32[36,128,128]{2,1,0:T(8,128)S(1)}, u32[]{:S(2)}) %copy-start.2) | copy-done | bytes 2359320
  26.7 0.0 copy-start.4
  26.7 0.0 copy-start.5
  26.7 0.0 copy-start.8
  26.7 1.3 %collective-permute-start.3 = (f32[12,128,128]{2,1,0:T(8,128)S(1)}, f32[12,128,128]{2,1,0:T(8,128)S(1)}, u32[]{:S(2)}, u32[]{:S(2)}) collective-permute-start(f32[12,128,128]{2,1,0:T(8,128)S(1)} %get-tuple-element.18), channel_id=1, source_target_pairs={{16,0},{48,32},{17,1},{49,33},{18,2},{50,34},{19,3},{51,35},{80,64... | collective-permute-start | bytes 2359304 | tf_op jit(solution)/shard_map/ppermute | solution.py:177
  28.0 2.9 %collective-permute-done.3 = f32[12,128,128]{2,1,0:T(8,128)S(1)} collective-permute-done((f32[12,128,128]{2,1,0:T(8,128)S(1)}, f32[12,128,128]{2,1,0:T(8,128)S(1)}, u32[]{:S(2)}, u32[]{:S(2)}) %collective-permute-start.3) | collective-permute-done | bytes 786464 | tf_op jit(solution)/shard_map/ppermute | solution.py:177
  30.8 1.0 slice_add_fusion.3
  31.9 0.0 copy-done.4
  31.9 0.0 copy-done.5
  31.9 0.0 copy-done.8
  31.9 0.0 copy-start.9
  31.9 1.4 %collective-permute-start.4 = (f32[36,128,128]{2,1,0:T(8,128)}, f32[36,128,128]{2,1,0:T(8,128)}, u32[]{:S(2)}, u32[]{:S(2)}) collective-permute-start(f32[36,128,128]{2,1,0:T(8,128)} %after.5), channel_id=1, source_target_pairs={{16,0},{48,32},{17,1},{49,33},{18,2},{50,34},{19,3},{51,35},{80,64... | collective-permute-start | bytes 7077896 | tf_op jit(solution)/shard_map/ppermute | solution.py:177
  33.3 6.8 %collective-permute-start.7 = (f32[12,128,128]{2,1,0:T(8,128)}, f32[12,128,128]{2,1,0:T(8,128)}, u32[]{:S(2)}, u32[]{:S(2)}) collective-permute-start(f32[12,128,128]{2,1,0:T(8,128)} %copy-done.8), channel_id=1, source_target_pairs={{0,240},{32,17},{1,241},{33,18},{2,242},{34,19},{3,243},{35,16},{6... | collective-permute-start | bytes 2359304 | tf_op jit(solution)/shard_map/ppermute | solution.py:177
  40.2 5.8 %collective-permute-start.5 = (f32[12,128,128]{2,1,0:T(8,128)S(1)}, f32[12,128,128]{2,1,0:T(8,128)}, u32[]{:S(2)}, u32[]{:S(2)}) collective-permute-start(f32[12,128,128]{2,1,0:T(8,128)S(1)} %get-tuple-element.18), channel_id=1, source_target_pairs={{0,243},{32,16},{1,240},{33,17},{2,241},{34,18},{3,242},{35,19},{6... | collective-permute-start | bytes 2359304 | tf_op jit(solution)/shard_map/ppermute | solution.py:177
  45.9 0.0 copy-done.9
  45.9 2.4 %collective-permute-start.9 = (f32[6,128,128]{2,1,0:T(8,128)S(1)}, f32[6,128,128]{2,1,0:T(8,128)}, u32[]{:S(2)}, u32[]{:S(2)}) collective-permute-start(f32[6,128,128]{2,1,0:T(8,128)S(1)} %copy-done.9), channel_id=1, source_target_pairs={{0,3},{16,19},{32,35},{48,51},{1,0},{17,16},{33,32},{49,48},{2,1},... | collective-permute-start | bytes 1179656 | tf_op jit(solution)/shard_map/ppermute | solution.py:177
  48.3 0.5 collective-permute-start.11
  48.8 6.6 %collective-permute-done.7.x_ref = f32[12,128,128]{2,1,0:T(8,128)} collective-permute-done((f32[12,128,128]{2,1,0:T(8,128)}, f32[12,128,128]{2,1,0:T(8,128)}, u32[]{:S(2)}, u32[]{:S(2)}) %collective-permute-start.7) | collective-permute-done | bytes 786464 | tf_op jit(solution)/shard_map/ppermute | solution.py:177
  55.4 8.0 %collective-permute-start.8 = (f32[12,128,128]{2,1,0:T(8,128)}, f32[12,128,128]{2,1,0:T(8,128)}, u32[]{:S(2)}, u32[]{:S(2)}) collective-permute-start(f32[12,128,128]{2,1,0:T(8,128)} %after.9), channel_id=1, source_target_pairs={{0,240},{32,17},{1,241},{33,18},{2,242},{34,19},{3,243},{35,16},{6... | collective-permute-start | bytes 2359304 | tf_op jit(solution)/shard_map/ppermute | solution.py:177
  63.4 1.1 collective-permute-done.5.x_ref
  64.6 10.4 %collective-permute-start.6 = (f32[12,128,128]{2,1,0:T(8,128)}, f32[12,128,128]{2,1,0:T(8,128)S(1)}, u32[]{:S(2)}, u32[]{:S(2)}) collective-permute-start(f32[12,128,128]{2,1,0:T(8,128)} %after.7), channel_id=1, source_target_pairs={{0,243},{32,16},{1,240},{33,17},{2,241},{34,18},{3,242},{35,19},{6... | collective-permute-start | bytes 2359304 | tf_op jit(solution)/shard_map/ppermute | solution.py:177
  75.0 0.0 collective-permute-done.11
  75.0 0.0 collective-permute-done.9
  75.0 0.0 collective-permute-done.4
  75.0 2.5 %fusion.1 = (f32[12,128,128]{2,1,0:T(8,128)S(1)}, f32[12,128,128]{2,1,0:T(8,128)S(1)}) fusion(f32[36,128,128]{2,1,0:T(8,128)} %collective-permute-done.4, f32[6,128,128]{2,1,0:T(8,128)} %collective-permute-done.9, f32[12,128,128]{2,1,0:T(8,128)S(1)} %get-tuple-element.23, f32[12,128,128]{2,1,0:T(8,128)} %after.6.first_ref, ...), kind=kLoop, calls=%fused_computation.3 | loop fusion | flops 1179648 | bytes 7077888 | tf_op jit(solution)/shard_map/add | solution.py:230
  77.6 2.4 %collective-permute-start.10 = (f32[12,128,128]{2,1,0:T(8,128)S(1)}, f32[12,128,128]{2,1,0:T(8,128)S(1)}, u32[]{:S(2)}, u32[]{:S(2)}) collective-permute-start(f32[12,128,128]{2,1,0:T(8,128)S(1)} %get-tuple-element.25), channel_id=1, source_target_pairs={{0,3},{16,19},{32,35},{48,51},{1,0},{17,16},{33,32},{49,48},{2,1},... | collective-permute-start | bytes 2359304 | tf_op jit(solution)/shard_map/ppermute | solution.py:177
  79.9 0.6 collective-permute-start.12
  80.6 0.5 collective-permute-done.8
  81.1 11.1 %collective-permute-done.6 = f32[12,128,128]{2,1,0:T(8,128)S(1)} collective-permute-done((f32[12,128,128]{2,1,0:T(8,128)}, f32[12,128,128]{2,1,0:T(8,128)S(1)}, u32[]{:S(2)}, u32[]{:S(2)}) %collective-permute-start.6) | collective-permute-done | bytes 786464 | tf_op jit(solution)/shard_map/ppermute | solution.py:177
  92.2 18.7 %collective-permute-done.10 = f32[12,128,128]{2,1,0:T(8,128)S(1)} collective-permute-done((f32[12,128,128]{2,1,0:T(8,128)S(1)}, f32[12,128,128]{2,1,0:T(8,128)S(1)}, u32[]{:S(2)}, u32[]{:S(2)}) %collective-permute-start.10) | collective-permute-done | bytes 786464 | tf_op jit(solution)/shard_map/ppermute | solution.py:177
  110.9 4.6 %collective-permute-done.12 = f32[12,128,128]{2,1,0:T(8,128)S(1)} collective-permute-done((f32[12,128,128]{2,1,0:T(8,128)S(1)}, f32[12,128,128]{2,1,0:T(8,128)S(1)}, u32[]{:S(2)}, u32[]{:S(2)}) %collective-permute-start.12) | collective-permute-done | bytes 786464 | tf_op jit(solution)/shard_map/ppermute | solution.py:177
  115.6 2.6 %fusion.6 = f32[1,1,12,128,128]{4,3,2,1,0:T(8,128)} fusion(f32[12,128,128]{2,1,0:T(8,128)S(1)} %collective-permute-done.12, f32[12,128,128]{2,1,0:T(8,128)S(1)} %collective-permute-done.10, f32[12,128,128]{2,1,0:T(8,128)} %collective-permute-done.8, f32[12,128,128]{2,1,0:T(8,128)S(1)} %collective-permute-done.6, f32[12,128,128]{2,1,0:T(8,128)S(1)} %get-tuple-element.15, ...), kind=kLoop, calls=%fused_computation.9 | loop fusion | flops 983040 | bytes 5505024 | tf_op jit(solution)/shard_map/reshape | solution.py:233
  (7 shorter events, 0.0 us)
Async XLA Ops:
  2.6 17.2 %collective-permute-start.2 = (f32[8,128,128]{2,1,0:T(8,128)}, f32[8,128,128]{2,1,0:T(8,128)S(1)}, u32[]{:S(2)}, u32[]{:S(2)}) collective-permute-start(f32[8,128,128]{2,1,0:T(8,128)} %pack_right.1.refs_4_), channel_id=1, source_target_pairs={{4,16},{8,20},{12,24},{0,28},{20,32},{24,36},{28,40},{16,44},{36,4... | collective-permute-start | bytes 1572872 | tf_op jit(solution)/shard_map/ppermute | solution.py:208
  3.5 16.3 %collective-permute-start = (s32[3,256]{1,0:T(4,128)S(1)}, s32[3,256]{1,0:T(4,128)S(1)}, u32[]{:S(2)}, u32[]{:S(2)}) collective-permute-start(s32[3,256]{1,0:T(4,128)S(1)} %bitcast.21), channel_id=1, source_target_pairs={{0,16},{16,32},{32,48},{48,64},{64,80},{80,96},{96,112},{112,128},... | collective-permute-start | bytes 9224 | tf_op jit(solution)/shard_map/ppermute | solution.py:210
  5.5 14.3 %collective-permute-start.1 = (s32[16]{0:T(128)}, s32[16]{0:T(128)S(1)}, u32[]{:S(2)}, u32[]{:S(2)}) collective-permute-start(s32[16]{0:T(128)} %bitcast.18), channel_id=1, source_target_pairs={{4,16},{8,20},{12,24},{0,28},{20,32},{24,36},{28,40},{16,44},{36,4... | collective-permute-start | bytes 200 | tf_op jit(solution)/shard_map/ppermute | solution.py:209
  8.2 4.6 %copy-start = (f32[1,1,1,192,128,128]{5,4,3,2,1,0:T(8,128)S(1)}, f32[1,1,1,192,128,128]{5,4,3,2,1,0:T(8,128)}, u32[]{:S(2)}) copy-start(f32[1,1,1,192,128,128]{5,4,3,2,1,0:T(8,128)} %param.5) | copy-start | bytes 37748740
  12.8 1.0 copy-start.3
  13.8 0.7 copy-start.6
  14.5 0.7 copy-start.7
  15.1 4.7 %copy-start.1 = (f32[1,1,1,192,128,128]{5,4,3,2,1,0:T(8,128)S(1)}, f32[1,1,1,192,128,128]{5,4,3,2,1,0:T(8,128)}, u32[]{:S(2)}) copy-start(f32[1,1,1,192,128,128]{5,4,3,2,1,0:T(8,128)} %param.5) | copy-start | bytes 37748740
  25.2 1.4 %copy-start.2 = (f32[36,128,128]{2,1,0:T(8,128)}, f32[36,128,128]{2,1,0:T(8,128)S(1)}, u32[]{:S(2)}) copy-start(f32[36,128,128]{2,1,0:T(8,128)S(1)} %get-tuple-element.17.x_ref) | copy-start | bytes 7077892
  26.7 5.2 %copy-start.4 = (f32[12,128,128]{2,1,0:T(8,128)}, f32[12,128,128]{2,1,0:T(8,128)S(1)}, u32[]{:S(2)}) copy-start(f32[12,128,128]{2,1,0:T(8,128)S(1)} %get-tuple-element.19.x_ref) | copy-start | bytes 2359300
  26.7 5.2 %copy-start.5 = (f32[12,128,128]{2,1,0:T(8,128)}, f32[12,128,128]{2,1,0:T(8,128)S(1)}, u32[]{:S(2)}) copy-start(f32[12,128,128]{2,1,0:T(8,128)S(1)} %get-tuple-element.20.x_ref) | copy-start | bytes 2359300
  26.7 5.2 %copy-start.8 = (f32[12,128,128]{2,1,0:T(8,128)}, f32[12,128,128]{2,1,0:T(8,128)S(1)}, u32[]{:S(2)}) copy-start(f32[12,128,128]{2,1,0:T(8,128)S(1)} %get-tuple-element.21) | copy-start | bytes 2359300
  26.7 4.2 %collective-permute-start.3 = (f32[12,128,128]{2,1,0:T(8,128)S(1)}, f32[12,128,128]{2,1,0:T(8,128)S(1)}, u32[]{:S(2)}, u32[]{:S(2)}) collective-permute-start(f32[12,128,128]{2,1,0:T(8,128)S(1)} %get-tuple-element.18), channel_id=1, source_target_pairs={{16,0},{48,32},{17,1},{49,33},{18,2},{50,34},{19,3},{51,35},{80,64... | collective-permute-start | bytes 2359304 | tf_op jit(solution)/shard_map/ppermute | solution.py:177
  31.9 14.1 %copy-start.9 = (f32[6,128,128]{2,1,0:T(8,128)S(1)}, f32[6,128,128]{2,1,0:T(8,128)}, u32[]{:S(2)}) copy-start(f32[6,128,128]{2,1,0:T(8,128)} %get-tuple-element.28.first_ref) | copy-start | bytes 1179652
  31.9 43.1 %collective-permute-start.4 = (f32[36,128,128]{2,1,0:T(8,128)}, f32[36,128,128]{2,1,0:T(8,128)}, u32[]{:S(2)}, u32[]{:S(2)}) collective-permute-start(f32[36,128,128]{2,1,0:T(8,128)} %after.5), channel_id=1, source_target_pairs={{16,0},{48,32},{17,1},{49,33},{18,2},{50,34},{19,3},{51,35},{80,64... | collective-permute-start | bytes 7077896 | tf_op jit(solution)/shard_map/ppermute | solution.py:177
  33.3 22.1 %collective-permute-start.7 = (f32[12,128,128]{2,1,0:T(8,128)}, f32[12,128,128]{2,1,0:T(8,128)}, u32[]{:S(2)}, u32[]{:S(2)}) collective-permute-start(f32[12,128,128]{2,1,0:T(8,128)} %copy-done.8), channel_id=1, source_target_pairs={{0,240},{32,17},{1,241},{33,18},{2,242},{34,19},{3,243},{35,16},{6... | collective-permute-start | bytes 2359304 | tf_op jit(solution)/shard_map/ppermute | solution.py:177
  40.2 24.4 %collective-permute-start.5 = (f32[12,128,128]{2,1,0:T(8,128)S(1)}, f32[12,128,128]{2,1,0:T(8,128)}, u32[]{:S(2)}, u32[]{:S(2)}) collective-permute-start(f32[12,128,128]{2,1,0:T(8,128)S(1)} %get-tuple-element.18), channel_id=1, source_target_pairs={{0,243},{32,16},{1,240},{33,17},{2,241},{34,18},{3,242},{35,19},{6... | collective-permute-start | bytes 2359304 | tf_op jit(solution)/shard_map/ppermute | solution.py:177
  45.9 29.1 %collective-permute-start.9 = (f32[6,128,128]{2,1,0:T(8,128)S(1)}, f32[6,128,128]{2,1,0:T(8,128)}, u32[]{:S(2)}, u32[]{:S(2)}) collective-permute-start(f32[6,128,128]{2,1,0:T(8,128)S(1)} %copy-done.9), channel_id=1, source_target_pairs={{0,3},{16,19},{32,35},{48,51},{1,0},{17,16},{33,32},{49,48},{2,1},... | collective-permute-start | bytes 1179656 | tf_op jit(solution)/shard_map/ppermute | solution.py:177
  48.3 26.7 %collective-permute-start.11 = (f32[6,128,128]{2,1,0:T(8,128)}, f32[6,128,128]{2,1,0:T(8,128)}, u32[]{:S(2)}, u32[]{:S(2)}) collective-permute-start(f32[6,128,128]{2,1,0:T(8,128)} %get-tuple-element.27.first_ref), channel_id=1, source_target_pairs={{0,1},{16,17},{32,33},{48,49},{1,2},{17,18},{33,34},{49,50},{2,3},... | collective-permute-start | bytes 1179656 | tf_op jit(solution)/shard_map/ppermute | solution.py:177
  55.4 25.7 %collective-permute-start.8 = (f32[12,128,128]{2,1,0:T(8,128)}, f32[12,128,128]{2,1,0:T(8,128)}, u32[]{:S(2)}, u32[]{:S(2)}) collective-permute-start(f32[12,128,128]{2,1,0:T(8,128)} %after.9), channel_id=1, source_target_pairs={{0,240},{32,17},{1,241},{33,18},{2,242},{34,19},{3,243},{35,16},{6... | collective-permute-start | bytes 2359304 | tf_op jit(solution)/shard_map/ppermute | solution.py:177
  64.6 27.6 %collective-permute-start.6 = (f32[12,128,128]{2,1,0:T(8,128)}, f32[12,128,128]{2,1,0:T(8,128)S(1)}, u32[]{:S(2)}, u32[]{:S(2)}) collective-permute-start(f32[12,128,128]{2,1,0:T(8,128)} %after.7), channel_id=1, source_target_pairs={{0,243},{32,16},{1,240},{33,17},{2,241},{34,18},{3,242},{35,19},{6... | collective-permute-start | bytes 2359304 | tf_op jit(solution)/shard_map/ppermute | solution.py:177
  77.6 33.4 %collective-permute-start.10 = (f32[12,128,128]{2,1,0:T(8,128)S(1)}, f32[12,128,128]{2,1,0:T(8,128)S(1)}, u32[]{:S(2)}, u32[]{:S(2)}) collective-permute-start(f32[12,128,128]{2,1,0:T(8,128)S(1)} %get-tuple-element.25), channel_id=1, source_target_pairs={{0,3},{16,19},{32,35},{48,51},{1,0},{17,16},{33,32},{49,48},{2,1},... | collective-permute-start | bytes 2359304 | tf_op jit(solution)/shard_map/ppermute | solution.py:177
  79.9 35.6 %collective-permute-start.12 = (f32[12,128,128]{2,1,0:T(8,128)S(1)}, f32[12,128,128]{2,1,0:T(8,128)S(1)}, u32[]{:S(2)}, u32[]{:S(2)}) collective-permute-start(f32[12,128,128]{2,1,0:T(8,128)S(1)} %get-tuple-element.26), channel_id=1, source_target_pairs={{0,1},{16,17},{32,33},{48,49},{1,2},{17,18},{33,34},{49,50},{2,3},... | collective-permute-start | bytes 2359304 | tf_op jit(solution)/shard_map/ppermute | solution.py:177

commit v3 on v2

--- a/solution.py
+++ b/solution.py
@@ -141,6 +141,7 @@
             pltpu.SMEM((most,), jnp.int32),
             pltpu.SemaphoreType.DMA((len(parts),)),
         ],
+        cost_estimate=pl.CostEstimate(flops=10**9 if far else 0, bytes_accessed=0, transcendentals=0),
         compiler_params=pltpu.CompilerParams(vmem_limit_bytes=26 * 2**20),
         name=name,
     )(table, a_live, b_live, a, b_kept, *first)
@@ -156,7 +157,7 @@
         in_specs=[pl.BlockSpec(memory_space=pl.ANY)] * 2,
         out_specs=pl.BlockSpec(memory_space=pl.ANY),
         input_output_aliases={0: 0},
-        cost_estimate=pl.CostEstimate(flops=flops, bytes_accessed=0, transcendentals=0),
+        cost_estimate=pl.CostEstimate(flops=flops, bytes_accessed=flops // 300, transcendentals=0),
         name="after",
     )(x, first)
 
@@ -173,8 +174,10 @@
     return pairs
 
 
-def send(x, rule):
-    return lax.ppermute(x, ("row", "rep"), moves(rule))
+def send(x, rule, name, flops):
+    with jax.named_scope(name):
+        x = lax.ppermute(x, ("row", "rep"), moves(rule))
+        return after(x, lax.axis_index("rep").reshape(1), flops) if flops else x
 
 
 def to_other_core(x, z, core):
@@ -205,30 +208,33 @@
     to_left = [(i * cols + (j + 1) % cols, (i + 1) % rows * cols + j) for i in range(rows) for j in range(cols)]
     next_row = [(i, (i + 1) % rows) for i in range(rows)]
     kept = pack_right(b, b_on)
-    kept_far = lax.ppermute(kept, ("row", "col"), to_left)
-    b_on_far = lax.ppermute(b_on, ("row", "col"), to_left)
-    table_far = lax.ppermute(tables[1], "row", next_row)
+    with jax.named_scope("right"):
+        kept_far = lax.ppermute(kept, ("row", "col"), to_left)
+    with jax.named_scope("right_live"):
+        b_on_far = lax.ppermute(b_on, ("row", "col"), to_left)
+    with jax.named_scope("table"):
+        table_far = lax.ppermute(tables[1], "row", next_row)
 
     shares_at = [(0, HALF), (HALF, HALF)] + [(k * SHARE, SHARE) for k in range(1, N_REP)]
     own0a, own0b, own_down, own_up, own_here = products(a, a_on, kept, b_on, tables[0], (), shares_at, False, "first")
     shares_at = [(k * SHARE, SHARE) for k in range(N_REP)] + [(SHARE, C_SLOTS - SHARE)]
     far0, far1, far2, far3, rest = products(a, a_on, kept_far, b_on_far, table_far, (own0a,), shares_at, True, "second")
-    odd_down = send(far0, to_owner_ring(-1))
-    odd_up = send(far2, to_owner_ring(1))
-    near0 = send(far0, to_other_core)
+    odd_down = send(far0, to_owner_ring(-1), "odd_down", 0)
+    odd_up = send(far2, to_owner_ring(1), "odd_up", 0)
+    near0 = send(far0, to_other_core, "near0", 0)
 
     down = own0a + near0[:HALF]
     up = own0b + near0[HALF:]
-    near = send(after(rest, down), to_other_core)
-    odd_down = after(odd_down, down, 5 * 10**9)
-    odd_up = after(odd_up, up, 5 * 10**9)
-    down = send(down, layers_on(-1, (0, 1)))
-    up = send(up, layers_on(1, (0, 1)))
-    late_down = send(after(far1, odd_down), to_owner_ring(-1))
-    late_up = send(after(far3, odd_up), to_owner_ring(1))
+    near = send(after(rest, down), to_other_core, "near", 10**10)
+    half_down = send(down, layers_on(-1, (0, 1)), "half_down", 0)
+    half_up = send(up, layers_on(1, (0, 1)), "half_up", 10**13)
     nothing = jnp.zeros((HALF, BS, BS), f32)
-    down = send(own_down + odd_down + near[:SHARE] + jnp.concatenate([down, nothing]), layers_on(-1, (0, 1)))
-    up = send(own_up + odd_up + near[SHARE : 2 * SHARE] + jnp.concatenate([nothing, up]), layers_on(1, (0, 1)))
+    late_down = send(after(far1, odd_down, 0), to_owner_ring(-1), "late_down", 0)
+    late_up = send(after(far3, odd_up, 10**10), to_owner_ring(1), "late_up", 0)
+    down = own_down + odd_down + near[:SHARE] + jnp.concatenate([half_down, nothing])
+    up = own_up + odd_up + near[SHARE : 2 * SHARE] + jnp.concatenate([nothing, half_up])
+    down = send(down, layers_on(-1, (0, 1)), "down", 0)
+    up = send(up, layers_on(1, (0, 1)), "up", 10**11)
     shares = own_here + near[2 * SHARE :] + late_down + late_up + down + up
     return shares.reshape(1, 1, SHARE, BS, BS)
 

time: 119 us -> 117 us (0.983)
  starting transfers between devices: 44.4 us -> 39.6 us
  waiting for transfers between devices: 45.6 us -> 47.5 us
    ppermute x10, starting transfers between devices: 39.6 us -> 34.8 us  [send(): x = lax.ppermute(x, ('row', 'rep'), moves(rule))]
    ppermute x10, waiting for transfers between devices: 45.6 us -> 47.5 us  [send(): x = lax.ppermute(x, ('row', 'rep'), moves(rule))]
    unnamed x22 -> x18, local copies, waits for them, and re-layouts: 8.4 us -> 8.7 us
  transfers between devices with their start and end apart: 13 -> 13, of which waited for: 7 -> 5; matrix products, arithmetic and copies ran while one was open for 3% -> 4% of each run, Pallas kernels for 4% -> 4%
where the time goes in v3:
time: 117 us; the launch traced here: 116 us
  waiting for transfers between devices  47.5 us (41%)
  starting transfers between devices  39.6 us (34%)
  Pallas kernels  12 us (10%)
  local copies, waits for them, and re-layouts  9.48 us (8%)
  other arithmetic  7.15 us (6%)
    ppermute x10, waiting for transfers between devices, send(): x = lax.ppermute(x, ('row', 'rep'), moves(rule))  47.5 us
    ppermute x10, starting transfers between devices, send(): x = lax.ppermute(x, ('row', 'rep'), moves(rule))  34.8 us
    pallas_call x2, Pallas kernels, products(): pl.pallas_call(kernel, out_shape=[jax.ShapeDtypeStruct((size, BS, BS), f3...  9.38 us
    unnamed x18, local copies, waits for them, and re-layouts  8.7 us
    add x1, other arithmetic, shards(): own_down + odd_down + near[:SHARE] + jnp.concatenate([half_down, nothing])  3.43 us
    reshape x1, other arithmetic, shards(): return shares.reshape(1, 1, SHARE, BS, BS)  2.83 us
    ppermute x1, starting transfers between devices, shards(): b_on_far = lax.ppermute(b_on, ('row', 'col'), to_left)  2.71 us
    pallas_call x1, Pallas kernels, pack_right(): pl.pallas_call(pack_kernel, out_shape=jax.ShapeDtypeStruct((B_KEEP, BS, B...  2.62 us
  transfers between devices with their start and end apart: 13, of which 5 were waited for; matrix products, arithmetic and copies ran while one was open for 4% of the time, Pallas kernels for 4%

profile of v3, /device:TPU:8, one launch (start us, length us, event | category | flops | bytes accessed | tf_op | source)
XLA Modules:
  0.0 115.9 jit_solution(7181366178232157450)
XLA Ops:
  0.0 2.6 %pack_right.1.refs_4_ = f32[8,128,128]{2,1,0:T(8,128)} custom-call(s32[16]{0:T(128)} %bitcast.18, f32[16,128,128]{2,1,0:T(8,128)} %bitcast.21), custom_call_target="tpu_custom_call" | custom-call | tf_op jit(solution)/shard_map/pack_right/pallas_call | solution.py:38
  2.6 0.1 collective-permute-start.2
  2.7 0.8 fusion.7
  3.5 2.0 %collective-permute-start = (s32[3,256]{1,0:T(4,128)S(1)}, s32[3,256]{1,0:T(4,128)S(1)}, u32[]{:S(2)}, u32[]{:S(2)}) collective-permute-start(s32[3,256]{1,0:T(4,128)S(1)} %bitcast.22), channel_id=1, source_target_pairs={{0,16},{16,32},{32,48},{48,64},{64,80},{80,96},{96,112},{112,128},... | collective-permute-start | bytes 9224 | tf_op jit(solution)/shard_map/table/ppermute | solution.py:216
  5.5 2.7 %collective-permute-start.1 = (s32[16]{0:T(128)}, s32[16]{0:T(128)S(1)}, u32[]{:S(2)}, u32[]{:S(2)}) collective-permute-start(s32[16]{0:T(128)} %bitcast.19), channel_id=1, source_target_pairs={{4,16},{8,20},{12,24},{0,28},{20,32},{24,36},{28,40},{16,44},{36,4... | collective-permute-start | bytes 200 | tf_op jit(solution)/shard_map/right_live/ppermute | solution.py:214
  8.2 0.0 copy-start
  8.2 4.6 %copy-done = f32[1,1,1,192,128,128]{5,4,3,2,1,0:T(8,128)S(1)} copy-done((f32[1,1,1,192,128,128]{5,4,3,2,1,0:T(8,128)S(1)}, f32[1,1,1,192,128,128]{5,4,3,2,1,0:T(8,128)}, u32[]{:S(2)}) %copy-start) | copy-done | bytes 12582936
  12.8 0.0 copy-start.3
  12.8 1.0 copy-done.3
  13.8 0.0 copy-start.5
  13.8 0.7 copy-done.5
  14.5 0.0 copy-start.6
  14.5 0.7 copy-done.6
  15.1 0.0 copy-start.1
  15.1 4.2 %first.1 = (f32[6,128,128]{2,1,0:T(8,128)S(1)}, f32[6,128,128]{2,1,0:T(8,128)S(1)}, f32[12,128,128]{2,1,0:T(8,128)S(1)}, f32[12,128,128]{2,1,0:T(8,128)S(1)}, f32[12,128,128]{2,1,0:T(8,128)S(1)}) custom-call(s32[3,256]{1,0:T(4,128)S(1)} %bitcast.15, s32[192]{0:T(256)S(1)} %bitcast.16, s32[16]{0:T(128)S(1)} %bitcast.20, f32[192,128,128]{2,1,0:T(8,128)S(1)} %bitcast.13, ...), custom_call_target="tpu_custom_call" | custom-call | tf_op jit(solution)/shard_map/first/pallas_call | solution.py:127
  19.4 0.0 collective-permute-done.1.refs_2_
  19.4 0.0 collective-permute-done.refs_0_
  19.4 0.0 collective-permute-done.2.refs_4_
  19.4 0.3 copy-done.1
  19.7 5.2 %second.1 = (f32[12,128,128]{2,1,0:T(8,128)S(1)}, f32[12,128,128]{2,1,0:T(8,128)S(1)}, f32[12,128,128]{2,1,0:T(8,128)}, f32[12,128,128]{2,1,0:T(8,128)S(1)}, f32[36,128,128]{2,1,0:T(8,128)S(1)}) custom-call(s32[3,256]{1,0:T(4,128)S(1)} %collective-permute-done.refs_0_, s32[192]{0:T(256)S(1)} %bitcast.17, s32[16]{0:T(128)S(1)} %collective-permute-done.1.refs_2_, ...), custom_call_target="tpu_custom_call" | custom-call | flops 1000000000 | tf_op jit(solution)/shard_map/second/pallas_call | solution.py:127
  24.9 0.0 copy-start.2
  24.9 1.4 %copy-done.2 = f32[36,128,128]{2,1,0:T(8,128)} copy-done((f32[36,128,128]{2,1,0:T(8,128)}, f32[36,128,128]{2,1,0:T(8,128)S(1)}, u32[]{:S(2)}) %copy-start.2) | copy-done | bytes 2359320
  26.3 0.0 copy-start.4
  26.3 0.0 copy-start.7
  26.3 1.3 %collective-permute-start.3 = (f32[12,128,128]{2,1,0:T(8,128)S(1)}, f32[12,128,128]{2,1,0:T(8,128)S(1)}, u32[]{:S(2)}, u32[]{:S(2)}) collective-permute-start(f32[12,128,128]{2,1,0:T(8,128)S(1)} %get-tuple-element.18), channel_id=1, source_target_pairs={{16,0},{48,32},{17,1},{49,33},{18,2},{50,34},{19,3},{51,35},{80,64... | collective-permute-start | bytes 2359304 | tf_op jit(solution)/shard_map/near0/ppermute | solution.py:179
  27.6 10.8 %collective-permute-start.5 = (f32[12,128,128]{2,1,0:T(8,128)S(1)}, f32[12,128,128]{2,1,0:T(8,128)}, u32[]{:S(2)}, u32[]{:S(2)}) collective-permute-start(f32[12,128,128]{2,1,0:T(8,128)S(1)} %get-tuple-element.18), channel_id=1, source_target_pairs={{0,243},{32,16},{1,240},{33,17},{2,241},{34,18},{3,242},{35,19},{6... | collective-permute-start | bytes 2359304 | tf_op jit(solution)/shard_map/odd_down/ppermute | solution.py:179
  38.4 0.0 collective-permute-done.3
  38.4 0.9 slice_add_fusion.3
  39.3 0.0 copy-done.4
  39.3 0.0 copy-done.7
  39.3 0.0 collective-permute-start.11
  39.3 2.2 %collective-permute-start.7 = (f32[12,128,128]{2,1,0:T(8,128)}, f32[12,128,128]{2,1,0:T(8,128)}, u32[]{:S(2)}, u32[]{:S(2)}) collective-permute-start(f32[12,128,128]{2,1,0:T(8,128)} %get-tuple-element.21), channel_id=1, source_target_pairs={{0,240},{32,17},{1,241},{33,18},{2,242},{34,19},{3,243},{35,16},{6... | collective-permute-start | bytes 2359304 | tf_op jit(solution)/shard_map/odd_up/ppermute | solution.py:179
  41.5 4.1 %collective-permute-start.9 = (f32[6,128,128]{2,1,0:T(8,128)}, f32[6,128,128]{2,1,0:T(8,128)}, u32[]{:S(2)}, u32[]{:S(2)}) collective-permute-start(f32[6,128,128]{2,1,0:T(8,128)} %get-tuple-element.28.first_ref), channel_id=1, source_target_pairs={{0,3},{16,19},{32,35},{48,51},{1,0},{17,16},{33,32},{49,48},{2,1},... | collective-permute-start | bytes 1179656 | tf_op jit(solution)/shard_map/half_down/ppermute | solution.py:179
  45.6 1.3 %collective-permute-start.4 = (f32[36,128,128]{2,1,0:T(8,128)}, f32[36,128,128]{2,1,0:T(8,128)}, u32[]{:S(2)}, u32[]{:S(2)}) collective-permute-start(f32[36,128,128]{2,1,0:T(8,128)} %after.6), channel_id=1, source_target_pairs={{16,0},{48,32},{17,1},{49,33},{18,2},{50,34},{19,3},{51,35},{80,64... | collective-permute-start | bytes 7077896 | tf_op jit(solution)/shard_map/near/ppermute | solution.py:179
  46.9 14.0 %collective-permute-done.5.first_ref = f32[12,128,128]{2,1,0:T(8,128)} collective-permute-done((f32[12,128,128]{2,1,0:T(8,128)S(1)}, f32[12,128,128]{2,1,0:T(8,128)}, u32[]{:S(2)}, u32[]{:S(2)}) %collective-permute-start.5) | collective-permute-done | bytes 786464 | tf_op jit(solution)/shard_map/odd_down/ppermute | solution.py:179
  60.9 9.6 %collective-permute-start.6 = (f32[12,128,128]{2,1,0:T(8,128)}, f32[12,128,128]{2,1,0:T(8,128)}, u32[]{:S(2)}, u32[]{:S(2)}) collective-permute-start(f32[12,128,128]{2,1,0:T(8,128)} %after.8), channel_id=1, source_target_pairs={{0,243},{32,16},{1,240},{33,17},{2,241},{34,18},{3,242},{35,19},{6... | collective-permute-start | bytes 2359304 | tf_op jit(solution)/shard_map/late_down/ppermute | solution.py:179
  70.5 0.0 collective-permute-done.11.x_ref
  70.5 0.0 collective-permute-done.4.x_ref
  70.5 0.0 collective-permute-done.7.first_ref
  70.5 0.0 collective-permute-done.9
  70.6 3.4 %fusion.1 = (f32[12,128,128]{2,1,0:T(8,128)S(1)}, f32[12,128,128]{2,1,0:T(8,128)}) fusion(f32[36,128,128]{2,1,0:T(8,128)} %after.7, f32[6,128,128]{2,1,0:T(8,128)} %collective-permute-done.9, f32[12,128,128]{2,1,0:T(8,128)S(1)} %get-tuple-element.22, f32[12,128,128]{2,1,0:T(8,128)} %collective-permute-done.5.first_ref, f32[6,128,128]{2,1,0:T(8,128)} %after.10, ...), kind=kLoop, calls=%fused_computation.3 | loop fusion | flops 1179648 | bytes 7077888 | tf_op jit(solution)/shard_map/add | solution.py:234
  74.0 0.0 collective-permute-start.12
  74.0 1.3 %collective-permute-start.8 = (f32[12,128,128]{2,1,0:T(8,128)}, f32[12,128,128]{2,1,0:T(8,128)S(1)}, u32[]{:S(2)}, u32[]{:S(2)}) collective-permute-start(f32[12,128,128]{2,1,0:T(8,128)} %after.9), channel_id=1, source_target_pairs={{0,240},{32,17},{1,241},{33,18},{2,242},{34,19},{3,243},{35,16},{6... | collective-permute-start | bytes 2359304 | tf_op jit(solution)/shard_map/late_up/ppermute | solution.py:179
  75.3 4.2 %collective-permute-start.10 = (f32[12,128,128]{2,1,0:T(8,128)S(1)}, f32[12,128,128]{2,1,0:T(8,128)S(1)}, u32[]{:S(2)}, u32[]{:S(2)}) collective-permute-start(f32[12,128,128]{2,1,0:T(8,128)S(1)} %get-tuple-element.25), channel_id=1, source_target_pairs={{0,3},{16,19},{32,35},{48,51},{1,0},{17,16},{33,32},{49,48},{2,1},... | collective-permute-start | bytes 2359304 | tf_op jit(solution)/shard_map/down/ppermute | solution.py:179
  79.5 24.1 %collective-permute-done.12.x_ref = f32[12,128,128]{2,1,0:T(8,128)} collective-permute-done((f32[12,128,128]{2,1,0:T(8,128)}, f32[12,128,128]{2,1,0:T(8,128)}, u32[]{:S(2)}, u32[]{:S(2)}) %collective-permute-start.12) | collective-permute-done | bytes 786464 | tf_op jit(solution)/shard_map/up/ppermute | solution.py:179
  103.6 0.3 collective-permute-done.6
  103.9 6.6 %collective-permute-done.8 = f32[12,128,128]{2,1,0:T(8,128)S(1)} collective-permute-done((f32[12,128,128]{2,1,0:T(8,128)}, f32[12,128,128]{2,1,0:T(8,128)S(1)}, u32[]{:S(2)}, u32[]{:S(2)}) %collective-permute-start.8) | collective-permute-done | bytes 786464 | tf_op jit(solution)/shard_map/late_up/ppermute | solution.py:179
  110.5 2.5 %collective-permute-done.10 = f32[12,128,128]{2,1,0:T(8,128)S(1)} collective-permute-done((f32[12,128,128]{2,1,0:T(8,128)S(1)}, f32[12,128,128]{2,1,0:T(8,128)S(1)}, u32[]{:S(2)}, u32[]{:S(2)}) %collective-permute-start.10) | collective-permute-done | bytes 786464 | tf_op jit(solution)/shard_map/down/ppermute | solution.py:179
  113.0 2.8 %fusion.6 = f32[1,1,12,128,128]{4,3,2,1,0:T(8,128)} fusion(f32[12,128,128]{2,1,0:T(8,128)} %after.11, f32[12,128,128]{2,1,0:T(8,128)S(1)} %collective-permute-done.10, f32[12,128,128]{2,1,0:T(8,128)S(1)} %collective-permute-done.8, f32[12,128,128]{2,1,0:T(8,128)} %collective-permute-done.6, f32[12,128,128]{2,1,0:T(8,128)S(1)} %get-tuple-element.15, ...), kind=kLoop, calls=%fused_computation.9 | loop fusion | flops 983040 | bytes 5505024 | tf_op jit(solution)/shard_map/reshape | solution.py:239
  (8 shorter events, 0.0 us)
Async XLA Ops:
  2.6 16.8 %collective-permute-start.2 = (f32[8,128,128]{2,1,0:T(8,128)}, f32[8,128,128]{2,1,0:T(8,128)S(1)}, u32[]{:S(2)}, u32[]{:S(2)}) collective-permute-start(f32[8,128,128]{2,1,0:T(8,128)} %pack_right.1.refs_4_), channel_id=1, source_target_pairs={{4,16},{8,20},{12,24},{0,28},{20,32},{24,36},{28,40},{16,44},{36,4... | collective-permute-start | bytes 1572872 | tf_op jit(solution)/shard_map/right/ppermute | solution.py:212
  3.5 15.9 %collective-permute-start = (s32[3,256]{1,0:T(4,128)S(1)}, s32[3,256]{1,0:T(4,128)S(1)}, u32[]{:S(2)}, u32[]{:S(2)}) collective-permute-start(s32[3,256]{1,0:T(4,128)S(1)} %bitcast.22), channel_id=1, source_target_pairs={{0,16},{16,32},{32,48},{48,64},{64,80},{80,96},{96,112},{112,128},... | collective-permute-start | bytes 9224 | tf_op jit(solution)/shard_map/table/ppermute | solution.py:216
  5.5 13.9 %collective-permute-start.1 = (s32[16]{0:T(128)}, s32[16]{0:T(128)S(1)}, u32[]{:S(2)}, u32[]{:S(2)}) collective-permute-start(s32[16]{0:T(128)} %bitcast.19), channel_id=1, source_target_pairs={{4,16},{8,20},{12,24},{0,28},{20,32},{24,36},{28,40},{16,44},{36,4... | collective-permute-start | bytes 200 | tf_op jit(solution)/shard_map/right_live/ppermute | solution.py:214
  8.2 4.6 %copy-start = (f32[1,1,1,192,128,128]{5,4,3,2,1,0:T(8,128)S(1)}, f32[1,1,1,192,128,128]{5,4,3,2,1,0:T(8,128)}, u32[]{:S(2)}) copy-start(f32[1,1,1,192,128,128]{5,4,3,2,1,0:T(8,128)} %param.5) | copy-start | bytes 37748740
  12.8 1.0 copy-start.3
  13.8 0.7 copy-start.5
  14.5 0.7 copy-start.6
  15.1 4.6 %copy-start.1 = (f32[1,1,1,192,128,128]{5,4,3,2,1,0:T(8,128)S(1)}, f32[1,1,1,192,128,128]{5,4,3,2,1,0:T(8,128)}, u32[]{:S(2)}) copy-start(f32[1,1,1,192,128,128]{5,4,3,2,1,0:T(8,128)} %param.5) | copy-start | bytes 37748740
  24.9 1.4 %copy-start.2 = (f32[36,128,128]{2,1,0:T(8,128)}, f32[36,128,128]{2,1,0:T(8,128)S(1)}, u32[]{:S(2)}) copy-start(f32[36,128,128]{2,1,0:T(8,128)S(1)} %get-tuple-element.17.x_ref) | copy-start | bytes 7077892
  26.3 13.0 %copy-start.4 = (f32[12,128,128]{2,1,0:T(8,128)}, f32[12,128,128]{2,1,0:T(8,128)S(1)}, u32[]{:S(2)}) copy-start(f32[12,128,128]{2,1,0:T(8,128)S(1)} %get-tuple-element.19.x_ref) | copy-start | bytes 2359300
  26.3 13.0 %copy-start.7 = (f32[12,128,128]{2,1,0:T(8,128)}, f32[12,128,128]{2,1,0:T(8,128)S(1)}, u32[]{:S(2)}) copy-start(f32[12,128,128]{2,1,0:T(8,128)S(1)} %get-tuple-element.20.x_ref) | copy-start | bytes 2359300
  26.3 12.1 %collective-permute-start.3 = (f32[12,128,128]{2,1,0:T(8,128)S(1)}, f32[12,128,128]{2,1,0:T(8,128)S(1)}, u32[]{:S(2)}, u32[]{:S(2)}) collective-permute-start(f32[12,128,128]{2,1,0:T(8,128)S(1)} %get-tuple-element.18), channel_id=1, source_target_pairs={{16,0},{48,32},{17,1},{49,33},{18,2},{50,34},{19,3},{51,35},{80,64... | collective-permute-start | bytes 2359304 | tf_op jit(solution)/shard_map/near0/ppermute | solution.py:179
  27.6 33.3 %collective-permute-start.5 = (f32[12,128,128]{2,1,0:T(8,128)S(1)}, f32[12,128,128]{2,1,0:T(8,128)}, u32[]{:S(2)}, u32[]{:S(2)}) collective-permute-start(f32[12,128,128]{2,1,0:T(8,128)S(1)} %get-tuple-element.18), channel_id=1, source_target_pairs={{0,243},{32,16},{1,240},{33,17},{2,241},{34,18},{3,242},{35,19},{6... | collective-permute-start | bytes 2359304 | tf_op jit(solution)/shard_map/odd_down/ppermute | solution.py:179
  39.3 31.2 %collective-permute-start.11 = (f32[6,128,128]{2,1,0:T(8,128)S(1)}, f32[6,128,128]{2,1,0:T(8,128)}, u32[]{:S(2)}, u32[]{:S(2)}) collective-permute-start(f32[6,128,128]{2,1,0:T(8,128)S(1)} %get-tuple-element.27), channel_id=1, source_target_pairs={{0,1},{16,17},{32,33},{48,49},{1,2},{17,18},{33,34},{49,50},{2,3},... | collective-permute-start | bytes 1179656 | tf_op jit(solution)/shard_map/half_up/ppermute | solution.py:179
  39.3 31.2 %collective-permute-start.7 = (f32[12,128,128]{2,1,0:T(8,128)}, f32[12,128,128]{2,1,0:T(8,128)}, u32[]{:S(2)}, u32[]{:S(2)}) collective-permute-start(f32[12,128,128]{2,1,0:T(8,128)} %get-tuple-element.21), channel_id=1, source_target_pairs={{0,240},{32,17},{1,241},{33,18},{2,242},{34,19},{3,243},{35,16},{6... | collective-permute-start | bytes 2359304 | tf_op jit(solution)/shard_map/odd_up/ppermute | solution.py:179
  41.5 29.0 %collective-permute-start.9 = (f32[6,128,128]{2,1,0:T(8,128)}, f32[6,128,128]{2,1,0:T(8,128)}, u32[]{:S(2)}, u32[]{:S(2)}) collective-permute-start(f32[6,128,128]{2,1,0:T(8,128)} %get-tuple-element.28.first_ref), channel_id=1, source_target_pairs={{0,3},{16,19},{32,35},{48,51},{1,0},{17,16},{33,32},{49,48},{2,1},... | collective-permute-start | bytes 1179656 | tf_op jit(solution)/shard_map/half_down/ppermute | solution.py:179
  45.6 24.9 %collective-permute-start.4 = (f32[36,128,128]{2,1,0:T(8,128)}, f32[36,128,128]{2,1,0:T(8,128)}, u32[]{:S(2)}, u32[]{:S(2)}) collective-permute-start(f32[36,128,128]{2,1,0:T(8,128)} %after.6), channel_id=1, source_target_pairs={{16,0},{48,32},{17,1},{49,33},{18,2},{50,34},{19,3},{51,35},{80,64... | collective-permute-start | bytes 7077896 | tf_op jit(solution)/shard_map/near/ppermute | solution.py:179
  60.9 43.0 %collective-permute-start.6 = (f32[12,128,128]{2,1,0:T(8,128)}, f32[12,128,128]{2,1,0:T(8,128)}, u32[]{:S(2)}, u32[]{:S(2)}) collective-permute-start(f32[12,128,128]{2,1,0:T(8,128)} %after.8), channel_id=1, source_target_pairs={{0,243},{32,16},{1,240},{33,17},{2,241},{34,18},{3,242},{35,19},{6... | collective-permute-start | bytes 2359304 | tf_op jit(solution)/shard_map/late_down/ppermute | solution.py:179
  74.0 29.6 %collective-permute-start.12 = (f32[12,128,128]{2,1,0:T(8,128)}, f32[12,128,128]{2,1,0:T(8,128)}, u32[]{:S(2)}, u32[]{:S(2)}) collective-permute-start(f32[12,128,128]{2,1,0:T(8,128)} %get-tuple-element.26), channel_id=1, source_target_pairs={{0,1},{16,17},{32,33},{48,49},{1,2},{17,18},{33,34},{49,50},{2,3},... | collective-permute-start | bytes 2359304 | tf_op jit(solution)/shard_map/up/ppermute | solution.py:179
  74.0 36.6 %collective-permute-start.8 = (f32[12,128,128]{2,1,0:T(8,128)}, f32[12,128,128]{2,1,0:T(8,128)S(1)}, u32[]{:S(2)}, u32[]{:S(2)}) collective-permute-start(f32[12,128,128]{2,1,0:T(8,128)} %after.9), channel_id=1, source_target_pairs={{0,240},{32,17},{1,241},{33,18},{2,242},{34,19},{3,243},{35,16},{6... | collective-permute-start | bytes 2359304 | tf_op jit(solution)/shard_map/late_up/ppermute | solution.py:179
  75.3 37.7 %collective-permute-start.10 = (f32[12,128,128]{2,1,0:T(8,128)S(1)}, f32[12,128,128]{2,1,0:T(8,128)S(1)}, u32[]{:S(2)}, u32[]{:S(2)}) collective-permute-start(f32[12,128,128]{2,1,0:T(8,128)S(1)} %get-tuple-element.25), channel_id=1, source_target_pairs={{0,3},{16,19},{32,35},{48,51},{1,0},{17,16},{33,32},{49,48},{2,1},... | collective-permute-start | bytes 2359304 | tf_op jit(solution)/shard_map/down/ppermute | solution.py:179

commit v4 on v3

--- a/solution.py
+++ b/solution.py
@@ -10,6 +10,7 @@
 B_KEEP = 8
 BATCH = 256
 UNROLL = 16
+RUN = 32
 N_ROW = 16
 N_REP = 4
 SHARE = C_SLOTS // N_REP
@@ -74,7 +75,15 @@
         target_list[n] = c + moved[(c * 43) >> 9]
         return n + jnp.where(c < C_SLOTS, a_live_ref[l] * b_live_ref[r], 0)
 
-    n = lax.fori_loop(0, BATCH, keep, 0, unroll=8)
+    def keep_run(k, n):
+        for u in range(RUN):
+            n = keep(k * RUN + u, n)
+        return n
+
+    runs = 0
+    for k in range(BATCH // RUN):
+        runs = runs + jnp.where(table_ref[2, k * RUN] < C_SLOTS, 1, 0)
+    n = lax.fori_loop(0, runs, keep_run, 0)
     for u in range(UNROLL):
         left_list[n + u] = 0
         right_list[n + u] = 0

time: 117 us -> 116 us (level); the launches traced: 116 us -> 116 us
  starting transfers between devices: 39.6 us -> 43.9 us
  Pallas kernels: 12 us -> 9.32 us
  waiting for transfers between devices: 47.5 us -> 45.1 us
  local copies, waits for them, and re-layouts: 9.48 us -> 10.8 us
    ppermute x10, starting transfers between devices: 34.8 us -> 39.1 us  [send(): x = lax.ppermute(x, ('row', 'rep'), moves(rule))]
    pallas_call x2, Pallas kernels: 9.38 us -> 6.69 us  [products(): pl.pallas_call(kernel, out_shape=[jax.ShapeDtypeStruct((size, BS, BS), f3...]
    ppermute x10, waiting for transfers between devices: 47.5 us -> 45.1 us  [send(): x = lax.ppermute(x, ('row', 'rep'), moves(rule))]
    unnamed x18, local copies, waits for them, and re-layouts: 8.7 us -> 10 us
  transfers between devices with their start and end apart: 13 -> 13, of which waited for: 5 -> 5; matrix products, arithmetic and copies ran while one was open for 4% -> 4% of each run, Pallas kernels for 4% -> 2%
where the time goes in v4:
time: 116 us
  waiting for transfers between devices  45.1 us (39%)
  starting transfers between devices  43.9 us (38%)
  local copies, waits for them, and re-layouts  10.8 us (9%)
  Pallas kernels  9.32 us (8%)
  other arithmetic  7.15 us (6%)
    ppermute x10, waiting for transfers between devices, send(): x = lax.ppermute(x, ('row', 'rep'), moves(rule))  45.1 us
    ppermute x10, starting transfers between devices, send(): x = lax.ppermute(x, ('row', 'rep'), moves(rule))  39.1 us
    unnamed x18, local copies, waits for them, and re-layouts  10 us
    pallas_call x2, Pallas kernels, products(): pl.pallas_call(kernel, out_shape=[jax.ShapeDtypeStruct((size, BS, BS), f3...  6.69 us
    add x1, other arithmetic, shards(): own_down + odd_down + near[:SHARE] + jnp.concatenate([half_down, nothing])  3.43 us
    reshape x1, other arithmetic, shards(): return shares.reshape(1, 1, SHARE, BS, BS)  2.83 us
    ppermute x1, starting transfers between devices, shards(): b_on_far = lax.ppermute(b_on, ('row', 'col'), to_left)  2.71 us
    pallas_call x1, Pallas kernels, pack_right(): pl.pallas_call(pack_kernel, out_shape=jax.ShapeDtypeStruct((B_KEEP, BS, B...  2.62 us
  transfers between devices with their start and end apart: 13, of which 5 were waited for; matrix products, arithmetic and copies ran while one was open for 4% of the time, Pallas kernels for 2%

profile of v4, /device:TPU:8, one launch (start us, length us, event | category | flops | bytes accessed | tf_op | source)
XLA Modules:
  0.0 116.3 jit_solution(278102239693240264)
XLA Ops:
  0.0 2.6 %pack_right.1.refs_4_ = f32[8,128,128]{2,1,0:T(8,128)} custom-call(s32[16]{0:T(128)} %bitcast.18, f32[16,128,128]{2,1,0:T(8,128)} %bitcast.21), custom_call_target="tpu_custom_call" | custom-call | tf_op jit(solution)/shard_map/pack_right/pallas_call | solution.py:39
  2.6 0.1 collective-permute-start.2
  2.7 0.8 fusion.7
  3.5 2.0 %collective-permute-start = (s32[3,256]{1,0:T(4,128)S(1)}, s32[3,256]{1,0:T(4,128)S(1)}, u32[]{:S(2)}, u32[]{:S(2)}) collective-permute-start(s32[3,256]{1,0:T(4,128)S(1)} %bitcast.22), channel_id=1, source_target_pairs={{0,16},{16,32},{32,48},{48,64},{64,80},{80,96},{96,112},{112,128},... | collective-permute-start | bytes 9224 | tf_op jit(solution)/shard_map/table/ppermute | solution.py:225
  5.5 2.7 %collective-permute-start.1 = (s32[16]{0:T(128)}, s32[16]{0:T(128)S(1)}, u32[]{:S(2)}, u32[]{:S(2)}) collective-permute-start(s32[16]{0:T(128)} %bitcast.19), channel_id=1, source_target_pairs={{4,16},{8,20},{12,24},{0,28},{20,32},{24,36},{28,40},{16,44},{36,4... | collective-permute-start | bytes 200 | tf_op jit(solution)/shard_map/right_live/ppermute | solution.py:223
  8.2 0.0 copy-start
  8.2 4.6 %copy-done = f32[1,1,1,192,128,128]{5,4,3,2,1,0:T(8,128)S(1)} copy-done((f32[1,1,1,192,128,128]{5,4,3,2,1,0:T(8,128)S(1)}, f32[1,1,1,192,128,128]{5,4,3,2,1,0:T(8,128)}, u32[]{:S(2)}) %copy-start) | copy-done | bytes 12582936
  12.8 0.0 copy-start.3
  12.8 1.0 copy-done.3
  13.8 0.0 copy-start.5
  13.8 0.7 copy-done.5
  14.5 0.0 copy-start.6
  14.5 0.7 copy-done.6
  15.1 0.0 copy-start.1
  15.1 2.9 %first.1 = (f32[6,128,128]{2,1,0:T(8,128)S(1)}, f32[6,128,128]{2,1,0:T(8,128)S(1)}, f32[12,128,128]{2,1,0:T(8,128)S(1)}, f32[12,128,128]{2,1,0:T(8,128)S(1)}, f32[12,128,128]{2,1,0:T(8,128)S(1)}) custom-call(s32[3,256]{1,0:T(4,128)S(1)} %bitcast.15, s32[192]{0:T(256)S(1)} %bitcast.16, s32[16]{0:T(128)S(1)} %bitcast.20, f32[192,128,128]{2,1,0:T(8,128)S(1)} %bitcast.13, ...), custom_call_target="tpu_custom_call" | custom-call | tf_op jit(solution)/shard_map/first/pallas_call | solution.py:136
  18.1 0.0 collective-permute-done.1.refs_2_
  18.1 0.0 collective-permute-done.refs_0_
  18.1 0.0 collective-permute-done.2.refs_4_
  18.1 1.6 %copy-done.1 = f32[1,1,1,192,128,128]{5,4,3,2,1,0:T(8,128)S(1)} copy-done((f32[1,1,1,192,128,128]{5,4,3,2,1,0:T(8,128)S(1)}, f32[1,1,1,192,128,128]{5,4,3,2,1,0:T(8,128)}, u32[]{:S(2)}) %copy-start.1) | copy-done | bytes 12582936
  19.7 3.8 %second.1 = (f32[12,128,128]{2,1,0:T(8,128)S(1)}, f32[12,128,128]{2,1,0:T(8,128)S(1)}, f32[12,128,128]{2,1,0:T(8,128)}, f32[12,128,128]{2,1,0:T(8,128)S(1)}, f32[36,128,128]{2,1,0:T(8,128)S(1)}) custom-call(s32[3,256]{1,0:T(4,128)S(1)} %collective-permute-done.refs_0_, s32[192]{0:T(256)S(1)} %bitcast.17, s32[16]{0:T(128)S(1)} %collective-permute-done.1.refs_2_, ...), custom_call_target="tpu_custom_call" | custom-call | flops 1000000000 | tf_op jit(solution)/shard_map/second/pallas_call | solution.py:136
  23.5 0.0 copy-start.2
  23.5 1.4 %copy-done.2 = f32[36,128,128]{2,1,0:T(8,128)} copy-done((f32[36,128,128]{2,1,0:T(8,128)}, f32[36,128,128]{2,1,0:T(8,128)S(1)}, u32[]{:S(2)}) %copy-start.2) | copy-done | bytes 2359320
  25.0 0.0 copy-start.4
  25.0 0.0 copy-start.7
  25.0 1.3 %collective-permute-start.3 = (f32[12,128,128]{2,1,0:T(8,128)S(1)}, f32[12,128,128]{2,1,0:T(8,128)S(1)}, u32[]{:S(2)}, u32[]{:S(2)}) collective-permute-start(f32[12,128,128]{2,1,0:T(8,128)S(1)} %get-tuple-element.18), channel_id=1, source_target_pairs={{16,0},{48,32},{17,1},{49,33},{18,2},{50,34},{19,3},{51,35},{80,64... | collective-permute-start | bytes 2359304 | tf_op jit(solution)/shard_map/near0/ppermute | solution.py:188
  26.3 12.4 %collective-permute-start.5 = (f32[12,128,128]{2,1,0:T(8,128)S(1)}, f32[12,128,128]{2,1,0:T(8,128)}, u32[]{:S(2)}, u32[]{:S(2)}) collective-permute-start(f32[12,128,128]{2,1,0:T(8,128)S(1)} %get-tuple-element.18), channel_id=1, source_target_pairs={{0,243},{32,16},{1,240},{33,17},{2,241},{34,18},{3,242},{35,19},{6... | collective-permute-start | bytes 2359304 | tf_op jit(solution)/shard_map/odd_down/ppermute | solution.py:188
  38.7 0.0 collective-permute-done.3
  38.7 0.9 slice_add_fusion.3
  39.6 0.0 copy-done.4
  39.6 0.0 copy-done.7
  39.6 0.0 collective-permute-start.11
  39.6 2.2 %collective-permute-start.7 = (f32[12,128,128]{2,1,0:T(8,128)}, f32[12,128,128]{2,1,0:T(8,128)}, u32[]{:S(2)}, u32[]{:S(2)}) collective-permute-start(f32[12,128,128]{2,1,0:T(8,128)} %get-tuple-element.21), channel_id=1, source_target_pairs={{0,240},{32,17},{1,241},{33,18},{2,242},{34,19},{3,243},{35,16},{6... | collective-permute-start | bytes 2359304 | tf_op jit(solution)/shard_map/odd_up/ppermute | solution.py:188
  41.8 4.1 %collective-permute-start.9 = (f32[6,128,128]{2,1,0:T(8,128)}, f32[6,128,128]{2,1,0:T(8,128)}, u32[]{:S(2)}, u32[]{:S(2)}) collective-permute-start(f32[6,128,128]{2,1,0:T(8,128)} %get-tuple-element.28.first_ref), channel_id=1, source_target_pairs={{0,3},{16,19},{32,35},{48,51},{1,0},{17,16},{33,32},{49,48},{2,1},... | collective-permute-start | bytes 1179656 | tf_op jit(solution)/shard_map/half_down/ppermute | solution.py:188
  45.9 1.3 %collective-permute-start.4 = (f32[36,128,128]{2,1,0:T(8,128)}, f32[36,128,128]{2,1,0:T(8,128)}, u32[]{:S(2)}, u32[]{:S(2)}) collective-permute-start(f32[36,128,128]{2,1,0:T(8,128)} %after.6), channel_id=1, source_target_pairs={{16,0},{48,32},{17,1},{49,33},{18,2},{50,34},{19,3},{51,35},{80,64... | collective-permute-start | bytes 7077896 | tf_op jit(solution)/shard_map/near/ppermute | solution.py:188
  47.2 14.2 %collective-permute-done.5.first_ref = f32[12,128,128]{2,1,0:T(8,128)} collective-permute-done((f32[12,128,128]{2,1,0:T(8,128)S(1)}, f32[12,128,128]{2,1,0:T(8,128)}, u32[]{:S(2)}, u32[]{:S(2)}) %collective-permute-start.5) | collective-permute-done | bytes 786464 | tf_op jit(solution)/shard_map/odd_down/ppermute | solution.py:188
  61.4 9.6 %collective-permute-start.6 = (f32[12,128,128]{2,1,0:T(8,128)}, f32[12,128,128]{2,1,0:T(8,128)}, u32[]{:S(2)}, u32[]{:S(2)}) collective-permute-start(f32[12,128,128]{2,1,0:T(8,128)} %after.8), channel_id=1, source_target_pairs={{0,243},{32,16},{1,240},{33,17},{2,241},{34,18},{3,242},{35,19},{6... | collective-permute-start | bytes 2359304 | tf_op jit(solution)/shard_map/late_down/ppermute | solution.py:188
  71.0 0.0 collective-permute-done.11.x_ref
  71.0 0.0 collective-permute-done.4.x_ref
  71.0 0.0 collective-permute-done.7.first_ref
  71.0 0.0 collective-permute-done.9
  71.0 3.4 %fusion.1 = (f32[12,128,128]{2,1,0:T(8,128)S(1)}, f32[12,128,128]{2,1,0:T(8,128)}) fusion(f32[36,128,128]{2,1,0:T(8,128)} %after.7, f32[6,128,128]{2,1,0:T(8,128)} %collective-permute-done.9, f32[12,128,128]{2,1,0:T(8,128)S(1)} %get-tuple-element.22, f32[12,128,128]{2,1,0:T(8,128)} %collective-permute-done.5.first_ref, f32[6,128,128]{2,1,0:T(8,128)} %after.10, ...), kind=kLoop, calls=%fused_computation.3 | loop fusion | flops 1179648 | bytes 7077888 | tf_op jit(solution)/shard_map/add | solution.py:243
  74.5 0.0 collective-permute-start.12
  74.5 1.3 %collective-permute-start.8 = (f32[12,128,128]{2,1,0:T(8,128)}, f32[12,128,128]{2,1,0:T(8,128)S(1)}, u32[]{:S(2)}, u32[]{:S(2)}) collective-permute-start(f32[12,128,128]{2,1,0:T(8,128)} %after.9), channel_id=1, source_target_pairs={{0,240},{32,17},{1,241},{33,18},{2,242},{34,19},{3,243},{35,16},{6... | collective-permute-start | bytes 2359304 | tf_op jit(solution)/shard_map/late_up/ppermute | solution.py:188
  75.8 6.9 %collective-permute-start.10 = (f32[12,128,128]{2,1,0:T(8,128)S(1)}, f32[12,128,128]{2,1,0:T(8,128)S(1)}, u32[]{:S(2)}, u32[]{:S(2)}) collective-permute-start(f32[12,128,128]{2,1,0:T(8,128)S(1)} %get-tuple-element.25), channel_id=1, source_target_pairs={{0,3},{16,19},{32,35},{48,51},{1,0},{17,16},{33,32},{49,48},{2,1},... | collective-permute-start | bytes 2359304 | tf_op jit(solution)/shard_map/down/ppermute | solution.py:188
  82.7 20.8 %collective-permute-done.12.x_ref = f32[12,128,128]{2,1,0:T(8,128)} collective-permute-done((f32[12,128,128]{2,1,0:T(8,128)}, f32[12,128,128]{2,1,0:T(8,128)}, u32[]{:S(2)}, u32[]{:S(2)}) %collective-permute-start.12) | collective-permute-done | bytes 786464 | tf_op jit(solution)/shard_map/up/ppermute | solution.py:188
  103.5 1.7 %collective-permute-done.6 = f32[12,128,128]{2,1,0:T(8,128)} collective-permute-done((f32[12,128,128]{2,1,0:T(8,128)}, f32[12,128,128]{2,1,0:T(8,128)}, u32[]{:S(2)}, u32[]{:S(2)}) %collective-permute-start.6) | collective-permute-done | bytes 786464 | tf_op jit(solution)/shard_map/late_down/ppermute | solution.py:188
  105.2 4.4 %collective-permute-done.8 = f32[12,128,128]{2,1,0:T(8,128)S(1)} collective-permute-done((f32[12,128,128]{2,1,0:T(8,128)}, f32[12,128,128]{2,1,0:T(8,128)S(1)}, u32[]{:S(2)}, u32[]{:S(2)}) %collective-permute-start.8) | collective-permute-done | bytes 786464 | tf_op jit(solution)/shard_map/late_up/ppermute | solution.py:188
  109.6 3.9 %collective-permute-done.10 = f32[12,128,128]{2,1,0:T(8,128)S(1)} collective-permute-done((f32[12,128,128]{2,1,0:T(8,128)S(1)}, f32[12,128,128]{2,1,0:T(8,128)S(1)}, u32[]{:S(2)}, u32[]{:S(2)}) %collective-permute-start.10) | collective-permute-done | bytes 786464 | tf_op jit(solution)/shard_map/down/ppermute | solution.py:188
  113.5 2.8 %fusion.6 = f32[1,1,12,128,128]{4,3,2,1,0:T(8,128)} fusion(f32[12,128,128]{2,1,0:T(8,128)} %after.11, f32[12,128,128]{2,1,0:T(8,128)S(1)} %collective-permute-done.10, f32[12,128,128]{2,1,0:T(8,128)S(1)} %collective-permute-done.8, f32[12,128,128]{2,1,0:T(8,128)} %collective-permute-done.6, f32[12,128,128]{2,1,0:T(8,128)S(1)} %get-tuple-element.15, ...), kind=kLoop, calls=%fused_computation.9 | loop fusion | flops 983040 | bytes 5505024 | tf_op jit(solution)/shard_map/reshape | solution.py:248
  (8 shorter events, 0.0 us)
Async XLA Ops:
  2.6 15.4 %collective-permute-start.2 = (f32[8,128,128]{2,1,0:T(8,128)}, f32[8,128,128]{2,1,0:T(8,128)S(1)}, u32[]{:S(2)}, u32[]{:S(2)}) collective-permute-start(f32[8,128,128]{2,1,0:T(8,128)} %pack_right.1.refs_4_), channel_id=1, source_target_pairs={{4,16},{8,20},{12,24},{0,28},{20,32},{24,36},{28,40},{16,44},{36,4... | collective-permute-start | bytes 1572872 | tf_op jit(solution)/shard_map/right/ppermute | solution.py:221
  3.5 14.6 %collective-permute-start = (s32[3,256]{1,0:T(4,128)S(1)}, s32[3,256]{1,0:T(4,128)S(1)}, u32[]{:S(2)}, u32[]{:S(2)}) collective-permute-start(s32[3,256]{1,0:T(4,128)S(1)} %bitcast.22), channel_id=1, source_target_pairs={{0,16},{16,32},{32,48},{48,64},{64,80},{80,96},{96,112},{112,128},... | collective-permute-start | bytes 9224 | tf_op jit(solution)/shard_map/table/ppermute | solution.py:225
  5.5 12.6 %collective-permute-start.1 = (s32[16]{0:T(128)}, s32[16]{0:T(128)S(1)}, u32[]{:S(2)}, u32[]{:S(2)}) collective-permute-start(s32[16]{0:T(128)} %bitcast.19), channel_id=1, source_target_pairs={{4,16},{8,20},{12,24},{0,28},{20,32},{24,36},{28,40},{16,44},{36,4... | collective-permute-start | bytes 200 | tf_op jit(solution)/shard_map/right_live/ppermute | solution.py:223
  8.2 4.6 %copy-start = (f32[1,1,1,192,128,128]{5,4,3,2,1,0:T(8,128)S(1)}, f32[1,1,1,192,128,128]{5,4,3,2,1,0:T(8,128)}, u32[]{:S(2)}) copy-start(f32[1,1,1,192,128,128]{5,4,3,2,1,0:T(8,128)} %param.5) | copy-start | bytes 37748740
  12.8 1.0 copy-start.3
  13.8 0.7 copy-start.5
  14.5 0.7 copy-start.6
  15.1 4.6 %copy-start.1 = (f32[1,1,1,192,128,128]{5,4,3,2,1,0:T(8,128)S(1)}, f32[1,1,1,192,128,128]{5,4,3,2,1,0:T(8,128)}, u32[]{:S(2)}) copy-start(f32[1,1,1,192,128,128]{5,4,3,2,1,0:T(8,128)} %param.5) | copy-start | bytes 37748740
  23.5 1.4 %copy-start.2 = (f32[36,128,128]{2,1,0:T(8,128)}, f32[36,128,128]{2,1,0:T(8,128)S(1)}, u32[]{:S(2)}) copy-start(f32[36,128,128]{2,1,0:T(8,128)S(1)} %get-tuple-element.17.x_ref) | copy-start | bytes 7077892
  25.0 14.6 %copy-start.4 = (f32[12,128,128]{2,1,0:T(8,128)}, f32[12,128,128]{2,1,0:T(8,128)S(1)}, u32[]{:S(2)}) copy-start(f32[12,128,128]{2,1,0:T(8,128)S(1)} %get-tuple-element.19.x_ref) | copy-start | bytes 2359300
  25.0 14.6 %copy-start.7 = (f32[12,128,128]{2,1,0:T(8,128)}, f32[12,128,128]{2,1,0:T(8,128)S(1)}, u32[]{:S(2)}) copy-start(f32[12,128,128]{2,1,0:T(8,128)S(1)} %get-tuple-element.20.x_ref) | copy-start | bytes 2359300
  25.0 13.7 %collective-permute-start.3 = (f32[12,128,128]{2,1,0:T(8,128)S(1)}, f32[12,128,128]{2,1,0:T(8,128)S(1)}, u32[]{:S(2)}, u32[]{:S(2)}) collective-permute-start(f32[12,128,128]{2,1,0:T(8,128)S(1)} %get-tuple-element.18), channel_id=1, source_target_pairs={{16,0},{48,32},{17,1},{49,33},{18,2},{50,34},{19,3},{51,35},{80,64... | collective-permute-start | bytes 2359304 | tf_op jit(solution)/shard_map/near0/ppermute | solution.py:188
  26.3 35.2 %collective-permute-start.5 = (f32[12,128,128]{2,1,0:T(8,128)S(1)}, f32[12,128,128]{2,1,0:T(8,128)}, u32[]{:S(2)}, u32[]{:S(2)}) collective-permute-start(f32[12,128,128]{2,1,0:T(8,128)S(1)} %get-tuple-element.18), channel_id=1, source_target_pairs={{0,243},{32,16},{1,240},{33,17},{2,241},{34,18},{3,242},{35,19},{6... | collective-permute-start | bytes 2359304 | tf_op jit(solution)/shard_map/odd_down/ppermute | solution.py:188
  39.6 31.4 %collective-permute-start.11 = (f32[6,128,128]{2,1,0:T(8,128)S(1)}, f32[6,128,128]{2,1,0:T(8,128)}, u32[]{:S(2)}, u32[]{:S(2)}) collective-permute-start(f32[6,128,128]{2,1,0:T(8,128)S(1)} %get-tuple-element.27), channel_id=1, source_target_pairs={{0,1},{16,17},{32,33},{48,49},{1,2},{17,18},{33,34},{49,50},{2,3},... | collective-permute-start | bytes 1179656 | tf_op jit(solution)/shard_map/half_up/ppermute | solution.py:188
  39.6 31.4 %collective-permute-start.7 = (f32[12,128,128]{2,1,0:T(8,128)}, f32[12,128,128]{2,1,0:T(8,128)}, u32[]{:S(2)}, u32[]{:S(2)}) collective-permute-start(f32[12,128,128]{2,1,0:T(8,128)} %get-tuple-element.21), channel_id=1, source_target_pairs={{0,240},{32,17},{1,241},{33,18},{2,242},{34,19},{3,243},{35,16},{6... | collective-permute-start | bytes 2359304 | tf_op jit(solution)/shard_map/odd_up/ppermute | solution.py:188
  41.8 29.2 %collective-permute-start.9 = (f32[6,128,128]{2,1,0:T(8,128)}, f32[6,128,128]{2,1,0:T(8,128)}, u32[]{:S(2)}, u32[]{:S(2)}) collective-permute-start(f32[6,128,128]{2,1,0:T(8,128)} %get-tuple-element.28.first_ref), channel_id=1, source_target_pairs={{0,3},{16,19},{32,35},{48,51},{1,0},{17,16},{33,32},{49,48},{2,1},... | collective-permute-start | bytes 1179656 | tf_op jit(solution)/shard_map/half_down/ppermute | solution.py:188
  45.9 25.1 %collective-permute-start.4 = (f32[36,128,128]{2,1,0:T(8,128)}, f32[36,128,128]{2,1,0:T(8,128)}, u32[]{:S(2)}, u32[]{:S(2)}) collective-permute-start(f32[36,128,128]{2,1,0:T(8,128)} %after.6), channel_id=1, source_target_pairs={{16,0},{48,32},{17,1},{49,33},{18,2},{50,34},{19,3},{51,35},{80,64... | collective-permute-start | bytes 7077896 | tf_op jit(solution)/shard_map/near/ppermute | solution.py:188
  61.4 43.7 %collective-permute-start.6 = (f32[12,128,128]{2,1,0:T(8,128)}, f32[12,128,128]{2,1,0:T(8,128)}, u32[]{:S(2)}, u32[]{:S(2)}) collective-permute-start(f32[12,128,128]{2,1,0:T(8,128)} %after.8), channel_id=1, source_target_pairs={{0,243},{32,16},{1,240},{33,17},{2,241},{34,18},{3,242},{35,19},{6... | collective-permute-start | bytes 2359304 | tf_op jit(solution)/shard_map/late_down/ppermute | solution.py:188
  74.5 29.0 %collective-permute-start.12 = (f32[12,128,128]{2,1,0:T(8,128)}, f32[12,128,128]{2,1,0:T(8,128)}, u32[]{:S(2)}, u32[]{:S(2)}) collective-permute-start(f32[12,128,128]{2,1,0:T(8,128)} %get-tuple-element.26), channel_id=1, source_target_pairs={{0,1},{16,17},{32,33},{48,49},{1,2},{17,18},{33,34},{49,50},{2,3},... | collective-permute-start | bytes 2359304 | tf_op jit(solution)/shard_map/up/ppermute | solution.py:188
  74.5 35.1 %collective-permute-start.8 = (f32[12,128,128]{2,1,0:T(8,128)}, f32[12,128,128]{2,1,0:T(8,128)S(1)}, u32[]{:S(2)}, u32[]{:S(2)}) collective-permute-start(f32[12,128,128]{2,1,0:T(8,128)} %after.9), channel_id=1, source_target_pairs={{0,240},{32,17},{1,241},{33,18},{2,242},{34,19},{3,243},{35,16},{6... | collective-permute-start | bytes 2359304 | tf_op jit(solution)/shard_map/late_up/ppermute | solution.py:188
  75.8 37.7 %collective-permute-start.10 = (f32[12,128,128]{2,1,0:T(8,128)S(1)}, f32[12,128,128]{2,1,0:T(8,128)S(1)}, u32[]{:S(2)}, u32[]{:S(2)}) collective-permute-start(f32[12,128,128]{2,1,0:T(8,128)S(1)} %get-tuple-element.25), channel_id=1, source_target_pairs={{0,3},{16,19},{32,35},{48,51},{1,0},{17,16},{33,32},{49,48},{2,1},... | collective-permute-start | bytes 2359304 | tf_op jit(solution)/shard_map/down/ppermute | solution.py:188
